TPU v7x, 32 devices: a whole 2x2x4 slice. The times are simulated.
32 devices in a mesh: tile: 8 (over z, y), layer: 4 (over x, core).
Axes of the slice: x: 2, y: 2, z: 4, core: 2. Of those that a mesh axis runs over, the one named last changes fastest.
Arguments:
- velocity_guess: float32 [2, 64, 3072], P(None, 'tile'), may hold values from -6 to 6
- hardness: float32 [16, 64, 3072], P('layer', 'tile'), may hold values from 0.7 to 1.5
- thickness: float32 [64, 3072], P('tile'), may hold values from 0.5 to 2
- friction: float32 [64, 3072], P('tile'), may hold values from 0.5 to 5
- grounded: int32 [64, 3072], P('tile'), may hold values 0 or 1
- ice_mask: int32 [64, 3072], P('tile'), may hold values 0 or 1
- driving: float32 [2, 64, 3072], P(None, 'tile'), may hold values from -8 to 8
- obs_cell: int32 [8, 4, 8, 512], P('tile', 'layer'), may hold values from 0 to 24575
- obs_east: float32 [8, 4, 8, 512], P('tile', 'layer'), may hold values from -6 to 6
- obs_north: float32 [8, 4, 8, 512], P('tile', 'layer'), may hold values from -6 to 6
- obs_weight: float32 [8, 4, 8, 512], P('tile', 'layer'), may hold values from 0.1 to 1
- obs_count: int32 [8, 4, 8], P('tile', 'layer'), may hold values from 64 to 512, as said below
Outputs:
- velocity: float32 [2, 64, 3072], P(None, 'tile')
- friction_gradient: float32 [64, 3072], P('tile')
Inputs may be any that keep to these rules, and one draw needn't show every extreme that they name: `obs_count`: counts lie between 64 and 512; in every draw one destination strip receives full blocks from every device. `obs_cell`: cells are numbered row by row within the destination strip.
All inputs are finite; a program needn't handle non-finite values. No bound on the sum of `grounded` or of `ice_mask` on one device may be relied on, other than what follows from the above.
Results may differ from a plain program's by a relative error of at most 0.00013.
Values sent between devices are 32-bit elements; how exact they have to be, the bound alone decides.
A program may use at most 64 MiB of HBM per device.

v0:
```python
import jax
import jax.numpy as jnp
from jax import lax
from jax.sharding import PartitionSpec as P

SWEEPS = 40


OMEGA = 0.5
REGULAR = 0.01


def padded(array, sides, width):
    for axis, dim in sides:
        count, length = (lax.axis_size(axis), array.shape[dim])
        up = [(i, (i + 1) % count) for i in range(count - 1)]
        down = [(j, i) for i, j in up]
        last = lax.slice_in_dim(array, length - width, length, axis=dim)
        leading = lax.slice_in_dim(array, 0, width, axis=dim)
        before = lax.ppermute(last, axis, up)
        after = lax.ppermute(leading, axis, down)
        array = jnp.concatenate([before, array, after], axis=dim)
    return array


def pad_cols(field):
    return jnp.pad(field, ((0, 0), (1, 1)))


def col_diff(field):
    wide = pad_cols(field)
    return 0.5 * (wide[:, 2:] - wide[:, :-2])


def row_diff(field):
    return 0.5 * (field[2:] - field[:-2])


def strain_rate(east_vel, north_vel):
    slope_ux = row_diff(east_vel)
    slope_vx = row_diff(north_vel)
    slope_uy = col_diff(east_vel[1:-1])
    slope_vy = col_diff(north_vel[1:-1])
    shear = slope_uy + slope_vx
    return (
        slope_ux * slope_ux
        + slope_vy * slope_vy
        + slope_ux * slope_vy
        + 0.25 * shear * shear
        + REGULAR
    )


def sweep(east_vel, north_vel, viscous, force_east, force_north, drag, inside):
    centre_visc = viscous[1:-1]
    wide_visc = pad_cols(centre_visc)
    face_north = 0.5 * (centre_visc + viscous[2:])
    face_south = 0.5 * (centre_visc + viscous[:-2])
    face_east = 0.5 * (centre_visc + wide_visc[:, 2:])
    face_west = 0.5 * (centre_visc + wide_visc[:, :-2])
    drag_mid = drag[1:-1]
    inside_mid = inside[1:-1]

    def laplace(field, row_gain, col_gain):
        centre = field[1:-1]
        wide = pad_cols(centre)
        rows_part = face_north * (centre - field[2:]) + face_south * (centre - field[:-2])
        cols_part = face_east * (centre - wide[:, 2:]) + face_west * (centre - wide[:, :-2])
        return row_gain * rows_part + col_gain * cols_part + drag_mid * centre

    cross_east = row_diff(2.0 * viscous * col_diff(north_vel)) + col_diff(
        centre_visc * row_diff(north_vel)
    )
    cross_north = col_diff(2.0 * centre_visc * row_diff(east_vel)) + row_diff(
        viscous * col_diff(east_vel)
    )
    resid_east = force_east[1:-1] - (laplace(east_vel, 4.0, 1.0) - cross_east)
    resid_north = force_north[1:-1] - (laplace(north_vel, 1.0, 4.0) - cross_north)
    diag_east = (
        4.0 * (face_north + face_south) + face_east + face_west + drag_mid + 1.0 - inside_mid
    )
    diag_north = (
        face_north + face_south + 4.0 * (face_east + face_west) + drag_mid + 1.0 - inside_mid
    )
    new_east = inside_mid * (east_vel[1:-1] + OMEGA * resid_east / diag_east)
    new_north = inside_mid * (north_vel[1:-1] + OMEGA * resid_north / diag_north)
    return jnp.stack([new_east, new_north], 0)


def relax(start, forces, viscous, drag, inside):

    def outer_single(step, fields):
        wide = padded(fields, (("tile", 1),), 1)
        return sweep(wide[0], wide[1], viscous, forces[0], forces[1], drag, inside)

    return lax.fori_loop(0, SWEEPS, outer_single, start)


def on_device(
    velocity_guess,
    hardness,
    thickness,
    friction,
    grounded,
    ice_mask,
    driving,
    obs_cell,
    obs_east,
    obs_north,
    obs_weight,
    obs_count,
):
    depth = 1
    rows_here = thickness.shape[0]
    cols_here = thickness.shape[1]
    drag = friction * grounded.astype(jnp.float32)
    inside = ice_mask.astype(jnp.float32)
    stacked = jnp.concatenate(
        [velocity_guess, thickness[None], drag[None], inside[None], driving, hardness], 0
    )
    extended = padded(stacked, (("tile", 1),), depth + 1)
    valid = (lax.broadcasted_iota(jnp.int32, obs_weight.shape, 3) < obs_count[..., None]).astype(
        jnp.float32
    )
    packed = jnp.stack([obs_cell.astype(jnp.float32), obs_east, obs_north, obs_weight * valid], 0)
    arrived = lax.all_to_all(packed, "tile", split_axis=3, concat_axis=1, tiled=True)
    rate = jnp.power(strain_rate(extended[0], extended[1]), -1.0 / 3.0)
    partial_sum = 0.5 * rate * jnp.sum(extended[7:, 1:-1], axis=0)
    layers_all = hardness.shape[0] * lax.axis_size("layer")
    cells = arrived[0].reshape(-1).astype(jnp.int32)
    weights = arrived[3].reshape(-1)
    total = lax.psum(partial_sum, "layer")
    viscous = extended[2, 1:-1] * total / layers_all
    drag_ext = extended[3, 1:-1]
    inside_ext = extended[4, 1:-1]
    forces = extended[5:7, 1:-1]
    velocity = relax(velocity_guess, forces, viscous, drag_ext, inside_ext)
    flat_east = velocity[0].reshape(-1)
    flat_north = velocity[1].reshape(-1)
    term_east = weights * (flat_east[cells] - arrived[1].reshape(-1))
    term_north = weights * (flat_north[cells] - arrived[2].reshape(-1))
    misfit_east = jax.ops.segment_sum(term_east, cells, num_segments=rows_here * cols_here)
    misfit_north = jax.ops.segment_sum(term_north, cells, num_segments=rows_here * cols_here)
    misfit_east, misfit_north = (misfit_east, misfit_north)
    summed = lax.psum((misfit_east, misfit_north), "layer")
    source = jnp.stack(
        [summed[0].reshape(rows_here, cols_here), summed[1].reshape(rows_here, cols_here)], 0
    )
    source_ext = jnp.pad(source, ((0, 0), (1, 1), (0, 0)))
    adjoint = relax(jnp.zeros_like(source), source_ext, viscous, drag_ext, inside_ext)
    drag_own = drag_ext[depth : depth + rows_here]
    gradient = -(drag_own * (velocity[0] * adjoint[0] + velocity[1] * adjoint[1]))
    return (velocity, gradient)


def solution(mesh):
    return jax.shard_map(
        on_device,
        mesh=mesh,
        in_specs=(
            P(None, "tile", None),
            P("layer", "tile", None),
            P("tile", None),
            P("tile", None),
            P("tile", None),
            P("tile", None),
            P(None, "tile", None),
            P("tile", "layer", None, None),
            P("tile", "layer", None, None),
            P("tile", "layer", None, None),
            P("tile", "layer", None, None),
            P("tile", "layer", None),
        ),
        out_specs=(P(None, "tile", None), P("tile", None)),
        check_vma=False,
    )
```

profile of v0, /device:TPU:0, one launch (start us, length us, event | category | flops | bytes accessed | tf_op | source)
XLA Modules:
  0.0 1014.0 jit_solution(14889470137017218762)
XLA Ops:
  11.9 7.3 all-to-all-start
  26.1 8.5 collective-permute-done.4
  38.7 32.4 %all-reduce.21.cloned.1.call-done = f32[10,3072]{1,0:T(8,128)} async-done(((f32[10,3072]{1,0:T(8,128)}), f32[10,3072]{1,0:T(8,128)}) %all-reduce.21.cloned.1.call-update) | async-done | bytes 122896 | tf_op jit(solution)/shard_map/psum | solution.py:132
  72.1 406.6 %while.24 = (s32[]{:T(128)}, f32[2,8,3072]{2,1,0:T(8,128)S(1)}, f32[10,3072]{1,0:T(8,128)S(1)}, f32[2,10,3072]{2,1,0:T(8,128)S(1)}, f32[8,3072]{1,0:T(8,128)S(1)...) while((s32[]{:T(128)}, f32[2,8,3072]{2,1,0:T(8,128)S(1)}, ...), condition=%wide.region_3.4_spmd, body=%wide.region_2.3_spmd.sunk | while | flops 2476034 | bytes 6734017 | solution.py:96
  77.1 4.2 collective-permute-done
  82.7 4.3 collective-permute-start.1
  88.5 4.2 collective-permute-done
  99.1 4.2 collective-permute-done
  104.7 4.3 collective-permute-start.1
  126.7 4.5 collective-permute-start.1
  223.1 4.2 collective-permute-done
  283.2 4.2 collective-permute-done
  363.3 4.5 collective-permute-done
  478.9 23.0 %gather_fusion = f32[4096]{0:T(1024)S(1)} fusion(f32[24576]{0:T(1024)S(1)} %bitcast.191, s32[4096]{0:T(1024)S(1)} %broadcast_clamp_fusion), kind=kCustom, calls=%fused_computation | custom fusion | bytes 49152 | tf_op jit(solution)/shard_map/gather | solution.py:140
  501.9 23.0 %gather_fusion.1 = f32[4096]{0:T(1024)S(1)} fusion(f32[24576]{0:T(1024)S(1)} %bitcast.192, s32[4096]{0:T(1024)S(1)} %broadcast_clamp_fusion), kind=kCustom, calls=%fused_computation.1 | custom fusion | bytes 49152 | tf_op jit(solution)/shard_map/gather | solution.py:141
  525.0 21.9 %scatter_custom_fusion = f32[24576]{0:T(1024)S(1)} fusion(s32[4096]{0:T(1024)S(1)} %bitcast.198, f32[4096]{0:T(1024)S(1)} %get-tuple-element.250, f32[]{:T(128)} %constant.91.clone.1), kind=kCustom, calls=%fused_computation.200 | custom fusion | flops 4096 | bytes 98308 | tf_op jit(solution)/shard_map/scatter-add | solution.py:142
  547.6 21.9 %scatter_custom_fusion.1 = f32[24576]{0:T(1024)S(1)} fusion(s32[4096]{0:T(1024)S(1)} %bitcast.199, f32[4096]{0:T(1024)S(1)} %get-tuple-element.251, f32[]{:T(128)} %constant.91.clone.1), kind=kCustom, calls=%fused_computation.198 | custom fusion | flops 4096 | bytes 98308 | tf_op jit(solution)/shard_map/scatter-add | solution.py:143
  570.2 28.6 %all-reduce.23.cloned.1.call-done = (f32[1,8,3072]{2,1,0:T(8,128)}, f32[1,8,3072]{2,1,0:T(8,128)}) async-done(((f32[1,8,3072]{2,1,0:T(8,128)}, f32[1,8,3072]{2,1,0:T(8,128)}), (f32[1,8,3072]{2,1,0:T(8,128)}, f32[1,8,3072]{2,1,0:T(8,128)})) %all-reduce.23.cloned.1.call-update) | async-done | bytes 196624 | tf_op jit(solution)/shard_map/psum | solution.py:145
  599.8 406.6 %while.25 = (s32[]{:T(128)}, f32[2,8,3072]{2,1,0:T(8,128)S(1)}, f32[10,3072]{1,0:T(8,128)S(1)}, f32[2,10,3072]{2,1,0:T(8,128)S(1)}, f32[8,3072]{1,0:T(8,128)S(1)...) while((s32[]{:T(128)}, f32[2,8,3072]{2,1,0:T(8,128)S(1)}, ...), condition=%wide.region_9.10_spmd, body=%wide.region_8.9_spmd.sunk | while | flops 2476034 | bytes 6734017 | solution.py:96
  610.4 4.3 collective-permute-start.3
  632.4 4.3 collective-permute-start.3
  654.4 4.3 collective-permute-start.3
  891.0 4.5 collective-permute-done.2
  980.9 4.2 collective-permute-done.2
  (1242 shorter events, 765.1 us)
Async XLA Ops:
  11.9 14.2 %all-to-all-start = ((f32[4,1,1,8,512]{4,2,1,0,3:T(1,128)}), f32[4,1,1,8,512]{4,2,1,0,3:T(1,128)S(1)}, u32[]{:S(2)}, u32[]{:S(2)}) async-start(f32[4,1,1,8,512]{4,2,1,0,3:T(1,128)} %pad_maximum_fusion.9), calls=%async_computation | async-start | bytes 131072 | tf_op jit(solution)/shard_map/all_to_all | solution.py:126
  19.2 51.9 %all-reduce.21.cloned.1.call-start = ((), (), s32[]{:S(2)}) async-start(), calls=%async_computation.1 | async-start | bytes 393216 | tf_op jit(solution)/shard_map/psum | solution.py:132
  19.6 15.0 %collective-permute-start.4 = (f32[11,2,3072]{2,1,0:T(2,128)S(1)}, f32[11,2,3072]{2,1,0:T(2,128)S(1)}, u32[]{:S(2)}, u32[]{:S(2)}) collective-permute-start(f32[11,2,3072]{2,1,0:T(2,128)S(1)} %get-tuple-element.240), channel_id=1, source_target_pairs={{0,4},{4,8},{8,12},{12,16},{16,20},{20,24},{24,28},{1,5},{5,9},{9,... | collective-permute-start | bytes 811016 | tf_op jit(solution)/shard_map/ppermute | solution.py:20
  23.5 11.1 %collective-permute-start.5 = (f32[11,2,3072]{2,1,0:T(2,128)S(1)}, f32[11,2,3072]{2,1,0:T(2,128)S(1)}, u32[]{:S(2)}, u32[]{:S(2)}) collective-permute-start(f32[11,2,3072]{2,1,0:T(2,128)S(1)} %get-tuple-element.241), channel_id=1, source_target_pairs={{4,0},{8,4},{12,8},{16,12},{20,16},{24,20},{28,24},{5,1},{9,5},{13... | collective-permute-start | bytes 811016 | tf_op jit(solution)/shard_map/ppermute | solution.py:21
  37.6 561.2 %all-reduce.23.cloned.1.call-start = ((), (), s32[]{:S(2)}) async-start(), calls=%async_computation.2 | async-start | bytes 393216 | tf_op jit(solution)/shard_map/psum | solution.py:145
  75.6 5.7 collective-permute-start
  82.7 5.8 collective-permute-start.1
  87.0 5.7 collective-permute-start
  104.7 5.8 collective-permute-start.1
  109.0 5.7 collective-permute-start
  126.7 6.1 collective-permute-start.1
  131.2 5.7 collective-permute-start
  151.5 5.7 collective-permute-start
  161.7 5.7 collective-permute-start
  191.7 5.7 collective-permute-start
  221.6 5.7 collective-permute-start
  251.8 5.7 collective-permute-start
  281.7 5.7 collective-permute-start
  361.8 6.0 collective-permute-start
  610.4 5.8 collective-permute-start.3
  632.4 5.8 collective-permute-start.3
  654.4 5.8 collective-permute-start.3
  658.7 5.7 collective-permute-start.2
  889.5 6.0 collective-permute-start.2
  (149 other events, 1310.8 us)
Sparse Core Ops, SparseCore 0:
  37.7 33.3 all-reduce.20
  570.3 28.4 all-reduce.22
where the time goes:
time: 1020 us; the launch traced here: 1010 us
  waiting for transfers between devices  421 us (41%)
  starting transfers between devices  356 us (35%)
  other arithmetic  129 us (13%)
  local copies, waits for them, and re-layouts  86 us (8%)
  between operations  14.4 us (1%)
    ppermute x81, waiting for transfers between devices, padded(): after = lax.ppermute(leading, axis, down)  338 us
    ppermute x81, starting transfers between devices, padded(): before = lax.ppermute(last, axis, up)  244 us
    ppermute x81, starting transfers between devices, padded(): after = lax.ppermute(leading, axis, down)  105 us
    another operation x240, other arithmetic, sweep(): return jnp.stack([new_east, new_north], 0)  43.9 us
    psum x1, waiting for transfers between devices, on_device(): total = lax.psum(partial_sum, 'layer')  32.4 us
    psum x1, waiting for transfers between devices, on_device(): summed = lax.psum((misfit_east, misfit_north), 'layer')  28.6 us
    concatenate x80, local copies, waits for them, and re-layouts, padded(): array = jnp.concatenate([before, array, after], axis=dim)  26.4 us
    gather x1, local copies, waits for them, and re-layouts, on_device(): term_east = weights * (flat_east[cells] - arrived[1].reshape(-1))  23 us
  transfers between devices with their start and end apart: 165, of which 164 were waited for; matrix products, arithmetic and copies ran while one was open for 0% of the time, Pallas kernels for 0%

commit v1 on v0

v1 whole, which is shorter than its diff:
```python
import functools

import jax
import jax.numpy as jnp
from jax import lax
from jax.experimental import pallas as pl
from jax.experimental.pallas import tpu as pltpu
from jax.sharding import PartitionSpec as P

SWEEPS = 40
OMEGA = 0.5
REGULAR = 0.01
HALO = 2 * SWEEPS
WIN = 256
LANES = 128
OFF = LANES - HALO
VMEM_LIMIT = 48 * 1024 * 1024


def scatter_maps(cell, east, north, weight, acc_ref, cols, first):
    blocks = cols // WIN
    slots = cell.shape[1]
    row = jnp.zeros_like(cell)
    for r in range(1, 8):
        row = row + jnp.where(cell >= r * cols, 1, 0)
    rem = cell - row * cols
    high = (rem // WIN) * 8 + row
    low = rem % WIN
    hit = lax.broadcasted_iota(jnp.int32, (8 * blocks, slots), 0) == high
    terms = []
    for value in (weight, weight * east, weight * north):
        rest = value
        for _ in range(3):
            part = rest.astype(jnp.bfloat16).astype(jnp.float32)
            rest = rest - part
            terms.append(jnp.where(hit, part, 0.0).astype(jnp.bfloat16))
    lhs = jnp.concatenate(terms, axis=0)
    rhs = jnp.where(
        lax.broadcasted_iota(jnp.int32, (WIN, slots), 0) == low, 1.0, 0.0
    ).astype(jnp.bfloat16)
    prod = lax.dot_general(
        lhs, rhs, (((1,), (1,)), ((), ())), preferred_element_type=jnp.float32
    )
    if first:
        acc_ref[...] = prod
    else:
        acc_ref[...] += prod


def maps_kernel(arr_ref, hard_ref, thick_ref, out_ref, acc_ref):
    cols = thick_ref.shape[1]
    blocks = cols // WIN
    hard = hard_ref[0]
    for k in range(1, hard_ref.shape[0]):
        hard = hard + hard_ref[k]
    out_ref[0] = hard * thick_ref[...]
    for s in range(arr_ref.shape[0]):
        scatter_maps(
            arr_ref[s, 0:1].astype(jnp.int32),
            arr_ref[s, 1:2],
            arr_ref[s, 2:3],
            arr_ref[s, 3:4],
            acc_ref,
            cols,
            s == 0,
        )
    n = 8 * blocks
    for v in range(3):
        for c in range(blocks):
            at = 3 * v * n + 8 * c
            out_ref[1 + v, :, c * WIN : (c + 1) * WIN] = (
                acc_ref[at : at + 8] + acc_ref[at + n : at + n + 8] + acc_ref[at + 2 * n : at + 2 * n + 8]
            )


def east_of(x):
    return pltpu.roll(x, WIN - 1, 1)


def west_of(x):
    return pltpu.roll(x, 1, 1)


def up(x):
    return pltpu.roll(x, x.shape[0] - 1, 0)


def down(x):
    return pltpu.roll(x, 1, 0)


def run_sweeps(state, coef, force):
    def wide(x):
        return (x, east_of(x), west_of(x))

    def rows(slot, a):
        return (wide(state[slot, 0, a]), wide(state[slot, 1, a]))

    def one(src, dst):
        first = rows(src, 0)
        last_u, last_v = state[src, 0, 7], state[src, 1, 7]
        before = (wide(down(last_u)), wide(down(last_v)))
        here = first
        for a in range(8):
            if a < 7:
                after = rows(src, a + 1)
            else:
                after = (wide(up(state[src, 0, 0])), wide(up(state[src, 1, 0])))
            for f in range(2):
                g = 1 - f
                c = lambda k: coef[f, k, a]
                new = c(0) * here[f][0] + force[f, a]
                new = new + c(1) * after[f][0]
                new = new + c(2) * before[f][0]
                new = new + c(3) * here[f][1]
                new = new + c(4) * here[f][2]
                new = new + c(5) * after[g][1]
                new = new + c(6) * after[g][2]
                new = new + c(7) * before[g][1]
                new = new + c(8) * before[g][2]
                state[dst, f, a] = new
            before, here = here, after

    def two(step, carry):
        one(0, 1)
        one(1, 0)
        return carry

    lax.fori_loop(0, SWEEPS // 2, two, 0)


def solve_kernel(layers, get, put, state, coef, gain, force):
    strips = state.shape[3]
    index = lax.broadcasted_iota(jnp.int32, (strips, WIN), 0)
    not_top = jnp.where(index == strips - 1, 0.0, 1.0)
    not_low = jnp.where(index == 0, 0.0, 1.0)

    def north(x, a):
        return x[a + 1] if a < 7 else up(x[0]) * not_top

    def south(x, a):
        return x[a - 1] if a > 0 else down(x[7]) * not_low

    u = [get(0, a) for a in range(8)]
    v = [get(1, a) for a in range(8)]
    visc = []
    for a in range(8):
        ux = 0.5 * (north(u, a) - south(u, a))
        vx = 0.5 * (north(v, a) - south(v, a))
        uy = 0.5 * (east_of(u[a]) - west_of(u[a]))
        vy = 0.5 * (east_of(v[a]) - west_of(v[a]))
        shear = uy + vx
        strain = ux * ux + vy * vy + ux * vy + 0.25 * shear * shear + REGULAR
        rate = jnp.exp(jnp.log(strain) * (-1.0 / 3.0))
        visc.append(0.5 * rate * get(6, a) / layers)
        state[0, 0, a] = u[a]
        state[0, 1, a] = v[a]
    for a in range(8):
        here = visc[a]
        vn, vs, ve, vw = north(visc, a), south(visc, a), east_of(here), west_of(here)
        fn, fs, fe, fw = (0.5 * (here + x) for x in (vn, vs, ve, vw))
        drag, inside = get(2, a), get(3, a)
        top = not_top if a == 7 else 1.0
        low = not_low if a == 0 else 1.0
        for f in range(2):
            rg, cg = (4.0, 1.0) if f == 0 else (1.0, 4.0)
            rx, cx = (0.5, 0.25) if f == 0 else (0.25, 0.5)
            spread = rg * (fn + fs) + cg * (fe + fw) + drag
            g = OMEGA * inside / (spread + 1.0 - inside)
            coef[f, 0, a] = inside - g * spread
            coef[f, 1, a] = g * rg * fn * top
            coef[f, 2, a] = g * rg * fs * low
            coef[f, 3, a] = g * cg * fe
            coef[f, 4, a] = g * cg * fw
            coef[f, 5, a] = g * (rx * vn + cx * ve) * top
            coef[f, 6, a] = -g * (rx * vn + cx * vw) * top
            coef[f, 7, a] = -g * (rx * vs + cx * ve) * low
            coef[f, 8, a] = g * (rx * vs + cx * vw) * low
            gain[f, a] = g
            force[f, a] = g * get(4 + f, a)
    run_sweeps(state, coef, force)
    for a in range(8):
        for f in range(2):
            vel = state[0, f, a]
            put(f, a, vel)
            force[f, a] = gain[f, a] * (vel * get(7, a) - get(8 + f, a))
            gain[f, a] = vel
            state[0, f, a] = jnp.zeros_like(vel)
    run_sweeps(state, coef, force)
    for a in range(8):
        put(2, a, -(get(2, a) * (gain[0, a] * state[0, 0, a] + gain[1, a] * state[0, 1, a])))


def solve_call(layers, x_ref, out_ref, state, coef, gain, force):
    def get(f, a):
        return x_ref[f, a]

    def put(f, a, value):
        out_ref[f, a] = pltpu.roll(value, WIN - HALO, 1)[:, :LANES]

    solve_kernel(layers, get, put, state, coef, gain, force)


def on_device(
    velocity_guess,
    hardness,
    thickness,
    friction,
    grounded,
    ice_mask,
    driving,
    obs_cell,
    obs_east,
    obs_north,
    obs_weight,
    obs_count,
):
    strips, parts = lax.axis_size("tile"), lax.axis_size("layer")
    cols = thickness.shape[1]
    group = cols // parts
    own = group // strips
    span = -(-(OFF + own * (strips - 1) + WIN) // LANES) * LANES
    layer = lax.axis_index("layer")
    drag = friction * grounded.astype(jnp.float32)
    inside = ice_mask.astype(jnp.float32)
    valid = (lax.broadcasted_iota(jnp.int32, obs_weight.shape, 3) < obs_count[..., None]).astype(
        jnp.float32
    )
    packed = jnp.stack(
        [obs_cell.astype(jnp.float32), obs_east, obs_north, obs_weight * valid], 0
    )[:, 0, 0]
    arrived = lax.all_to_all(packed.swapaxes(0, 1), "tile", split_axis=0, concat_axis=0, tiled=True)
    maps = pl.pallas_call(
        maps_kernel,
        out_shape=jax.ShapeDtypeStruct((4, 8, cols), jnp.float32),
        scratch_shapes=[pltpu.VMEM((9 * 8 * (cols // WIN), WIN), jnp.float32)],
        compiler_params=pltpu.CompilerParams(vmem_limit_bytes=VMEM_LIMIT),
    )(arrived, hardness, thickness)
    right = (parts - 1) * group + span - LANES - cols

    def pad(x):
        return jnp.pad(x, ((0, 0), (0, 0), (LANES, right)))

    def windows(x):
        return jnp.stack([x[:, :, OFF + own * t : OFF + own * t + WIN] for t in range(strips)], 0)

    maps = pad(maps)
    shares = jnp.stack([maps[:, :, group * p : group * p + span] for p in range(parts)], 0)
    summed = lax.psum_scatter(shares, "layer", scatter_dimension=0, tiled=False)
    plain = pad(jnp.concatenate([velocity_guess, drag[None], inside[None], driving], 0))
    plain = lax.dynamic_slice_in_dim(plain, layer * group, span, axis=2)
    send = windows(jnp.concatenate([plain, summed], 0))
    got = lax.all_to_all(send, "tile", split_axis=0, concat_axis=0, tiled=True)
    block = got.transpose(1, 2, 0, 3)
    result = pl.pallas_call(
        functools.partial(solve_call, float(hardness.shape[0] * parts)),
        out_shape=jax.ShapeDtypeStruct((3, 8, strips, LANES), jnp.float32),
        scratch_shapes=[
            pltpu.VMEM((2, 2, 8, strips, WIN), jnp.float32),
            pltpu.VMEM((2, 9, 8, strips, WIN), jnp.float32),
            pltpu.VMEM((2, 8, strips, WIN), jnp.float32),
            pltpu.VMEM((2, 8, strips, WIN), jnp.float32),
        ],
        compiler_params=pltpu.CompilerParams(vmem_limit_bytes=VMEM_LIMIT),
    )(block)
    back = lax.all_to_all(result.transpose(2, 0, 1, 3), "tile", split_axis=0, concat_axis=0, tiled=True)
    mine = back[..., :own].transpose(1, 2, 0, 3).reshape(3, 8, group)
    full = lax.all_gather(mine, "layer", axis=2, tiled=True)
    return full[:2], full[2]


def solution(mesh):
    return jax.shard_map(
        on_device,
        mesh=mesh,
        in_specs=(
            P(None, "tile", None),
            P("layer", "tile", None),
            P("tile", None),
            P("tile", None),
            P("tile", None),
            P("tile", None),
            P(None, "tile", None),
            P("tile", "layer", None, None),
            P("tile", "layer", None, None),
            P("tile", "layer", None, None),
            P("tile", "layer", None, None),
            P("tile", "layer", None),
        ),
        out_specs=(P(None, "tile", None), P("tile", None)),
        check_vma=False,
    )
```

time: 1020 us -> 110 us (0.11)
  waiting for transfers between devices: 421 us -> 17.4 us
  starting transfers between devices: 356 us -> 0.04 us
  other arithmetic: 129 us -> 4.05 us
  local copies, waits for them, and re-layouts: 86 us -> 5.41 us
  blocking collectives: 0 us -> 53 us
  Pallas kernels: 0 us -> 15 us
    ppermute x162 -> x0, waiting for transfers between devices: 359 us -> none  [the longest x81 338 us: padded(): after = lax.ppermute(leading, axis, down)]
    ppermute x162 -> x0, starting transfers between devices: 348 us -> none  [the longest x81 244 us: padded(): before = lax.ppermute(last, axis, up)]
    psum x2 -> x0, waiting for transfers between devices: 61.1 us -> none  [the longest x1 32.4 us: on_device(): total = lax.psum(partial_sum, 'layer')]
    all_to_all x0 -> x3, blocking collectives: none -> 47.2 us  [the longest x1 23 us: on_device(): got = lax.all_to_all(send, 'tile', split_axis=0, concat_axis=0, tiled=True)]
    gather x2 -> x0, local copies, waits for them, and re-layouts: 46.1 us -> none  [the longest x1 23 us: on_device(): term_east = weights * (flat_east[cells] - arrived[1].reshape(-1))]
    another operation x241 -> x2, other arithmetic: 44.9 us -> 0.91 us  [the longest x1 0.83 us: on_device(): jnp.stack([maps[:, :, group * p:group * p + span] for p in range(parts)], 0)]
    scatter-add x2 -> x0, other arithmetic: 43.8 us -> none  [the longest x1 21.9 us: on_device(): jax.ops.segment_sum(term_east, cells, num_segments=rows_here * cols_here)]
    mul x162 -> x0, other arithmetic: 30.1 us -> none  [the longest x80 22.2 us: sweep(): 2.0 * viscous * col_diff(north_vel)]
  transfers between devices with their start and end apart: 165 -> 1, of which waited for: 164 -> 1; matrix products, arithmetic and copies ran while one was open for 0% -> 0% of each run, Pallas kernels for 0% -> 0%
where the time goes in v1:
time: 110 us; the launch traced here: 109 us
  blocking collectives  53 us (48%)
  waiting for transfers between devices  17.4 us (16%)
  Pallas kernels  15 us (14%)
  between operations  14.2 us (13%)
  local copies, waits for them, and re-layouts  5.41 us (5%)
  other arithmetic  4.05 us (4%)
    all_to_all x1, blocking collectives, on_device(): got = lax.all_to_all(send, 'tile', split_axis=0, concat_axis=0, tiled=True)  23 us
    reduce_scatter x1, waiting for transfers between devices, on_device(): summed = lax.psum_scatter(shares, 'layer', scatter_dimension=0, tiled=False)  17.4 us
    all_to_all x1, blocking collectives, on_device(): lax.all_to_all(packed.swapaxes(0, 1), 'tile', split_axis=0, concat_axis=0...  14 us
    pallas_call x1, Pallas kernels, on_device(): pl.pallas_call(functools.partial(solve_call, float(hardness.shape[0] * pa...  12.9 us
    all_to_all x1, blocking collectives, on_device(): lax.all_to_all(result.transpose(2, 0, 1, 3), 'tile', split_axis=0, concat...  10.2 us
    all_gather x1, blocking collectives, on_device(): full = lax.all_gather(mine, 'layer', axis=2, tiled=True)  5.88 us
    unnamed x18, local copies, waits for them, and re-layouts  2.77 us
  transfers between devices with their start and end apart: 1, of which 1 were waited for; matrix products, arithmetic and copies ran while one was open for 0% of the time, Pallas kernels for 0%

profile of v1, /device:TPU:0, one launch (start us, length us, event | category | flops | bytes accessed | tf_op | source)
XLA Modules:
  0.0 109.1 jit_solution(10570251866744966756)
XLA Ops:
  7.2 0.8 convert_element_type.17
  8.0 0.7 stack.59
  8.7 0.8 fusion.35
  9.6 14.0 %all_to_all.15.arr_ref = f32[8,4,512]{2,1,0:T(4,128)S(1)} all-to-all(f32[8,4,512]{2,1,0:T(4,128)S(1)} %maximum_bitcast_fusion), channel_id=1, replica_groups=mesh['tile'=8,'layer'=4] {'tile'}, dimensions={0} | all-to-all | bytes 131072 | tf_op jit(solution)/shard_map/all_to_all | solution.py:232
  23.6 0.9 copy-done.1
  24.5 2.1 %shard_map.134 = f32[4,8,3072]{2,1,0:T(8,128)S(1)} custom-call(f32[8,4,512]{2,1,0:T(4,128)S(1)} %all_to_all.15.arr_ref, f32[4,8,3072]{2,1,0:T(8,128)S(1)} %copy-done, f32[8,3072]{1,0:T(8,128)S(1)} %copy-done.1), custom_call_target="tpu_custom_call" | custom-call | tf_op jit(solution)/shard_map/pallas_call | solution.py:233
  26.6 0.8 pad_maximum_fusion
  27.5 0.9 copy-done.5
  28.4 0.8 copy-done.4
  29.3 0.1 copy-done.3
  29.4 17.4 %reduce-scatter.2.cloned.1.call-done = f32[1,4,8,1024]{3,2,1,0:T(8,128)} async-done(((f32[4,4,8,1024]{3,2,1,0:T(8,128)}), f32[1,4,8,1024]{3,2,1,0:T(8,128)}) %reduce-scatter.2.cloned.1.call-update) | async-done | bytes 131088 | tf_op jit(solution)/shard_map/reduce_scatter | solution.py:249
  46.8 0.9 fusion.17
  47.8 0.1 fusion.23
  47.9 0.1 fusion.26
  48.0 0.1 fusion.29
  48.1 0.1 fusion.32
  48.4 23.0 %all_to_all.16 = f32[8,10,8,256]{3,2,1,0:T(8,128)S(1)} all-to-all(f32[8,10,8,256]{3,2,1,0:T(8,128)S(1)} %fusion.34), channel_id=1, replica_groups=mesh['tile'=8,'layer'=4] {'tile'}, dimensions={0} | all-to-all | bytes 1310720 | tf_op jit(solution)/shard_map/all_to_all | solution.py:253
  71.4 0.4 copy.36
  71.8 12.9 %shard_map.135 = f32[3,8,8,128]{3,2,1,0:T(8,128)S(1)} custom-call(f32[10,8,8,256]{3,2,1,0:T(8,128)S(1)} %bitcast.68), custom_call_target="tpu_custom_call" | custom-call | tf_op jit(solution)/shard_map/pallas_call | solution.py:255
  84.8 10.2 %all_to_all.17 = f32[8,3,8,128]{3,2,1,0:T(8,128)S(1)} all-to-all(f32[8,3,8,128]{3,2,1,0:T(8,128)S(1)} %copy.30), channel_id=1, replica_groups=mesh['tile'=8,'layer'=4] {'tile'}, dimensions={0} | all-to-all | bytes 196608 | tf_op jit(solution)/shard_map/all_to_all | solution.py:266
  94.9 0.1 reshape.42
  95.0 5.9 %all_gather.3 = f32[3,8,3072]{2,1,0:T(8,128)S(1)} all-gather(f32[3,8,768]{2,1,0:T(8,128)S(1)} %reshape.42), channel_id=1, replica_groups=mesh['tile'=8,'layer'=4] {'layer'}, dimensions={2}, use_global_device_ids=true | all-gather | bytes 368640 | tf_op jit(solution)/shard_map/all_gather | solution.py:268
  100.9 0.6 slice_bitcast_fusion.2
  101.6 0.7 slice.79
  (28 shorter events, 0.6 us)
Async XLA Ops:
  7.2 0.8 copy-start.8
  7.2 16.4 %copy-start = (f32[4,8,3072]{2,1,0:T(8,128)S(1)}, f32[4,8,3072]{2,1,0:T(8,128)}, u32[]{:S(2)}) copy-start(f32[4,8,3072]{2,1,0:T(8,128)} %hard_ref.1) | copy-start | bytes 1179652
  7.2 39.6 %reduce-scatter.2.cloned.1.call-start = ((), (), s32[]{:S(2)}) async-start(), calls=%async_computation.4 | async-start | bytes 655360 | tf_op jit(solution)/shard_map/reduce_scatter | solution.py:249
  23.6 0.9 copy-start.1
  27.4 0.9 copy-start.5
  27.4 0.9 copy-start.6
  27.4 1.0 copy-start.7
  28.3 0.9 copy-start.4
  28.3 1.0 copy-start.3
  46.8 1.0 copy-start.2
Sparse Core Ops, SparseCore 0:
  27.6 19.1 reduce-scatter.1

commit v2 on v1

--- a/solution.py
+++ b/solution.py
@@ -47,32 +47,6 @@
         acc_ref[...] += prod
 
 
-def maps_kernel(arr_ref, hard_ref, thick_ref, out_ref, acc_ref):
-    cols = thick_ref.shape[1]
-    blocks = cols // WIN
-    hard = hard_ref[0]
-    for k in range(1, hard_ref.shape[0]):
-        hard = hard + hard_ref[k]
-    out_ref[0] = hard * thick_ref[...]
-    for s in range(arr_ref.shape[0]):
-        scatter_maps(
-            arr_ref[s, 0:1].astype(jnp.int32),
-            arr_ref[s, 1:2],
-            arr_ref[s, 2:3],
-            arr_ref[s, 3:4],
-            acc_ref,
-            cols,
-            s == 0,
-        )
-    n = 8 * blocks
-    for v in range(3):
-        for c in range(blocks):
-            at = 3 * v * n + 8 * c
-            out_ref[1 + v, :, c * WIN : (c + 1) * WIN] = (
-                acc_ref[at : at + 8] + acc_ref[at + n : at + n + 8] + acc_ref[at + 2 * n : at + 2 * n + 8]
-            )
-
-
 def east_of(x):
     return pltpu.roll(x, WIN - 1, 1)
 
@@ -89,7 +63,7 @@
     return pltpu.roll(x, 1, 0)
 
 
-def run_sweeps(state, coef, force):
+def run_sweeps(state, coef, force, count):
     def wide(x):
         return (x, east_of(x), west_of(x))
 
@@ -126,10 +100,10 @@
         one(1, 0)
         return carry
 
-    lax.fori_loop(0, SWEEPS // 2, two, 0)
-
-
-def solve_kernel(layers, get, put, state, coef, gain, force):
+    lax.fori_loop(0, count // 2, two, 0)
+
+
+def make_coefs(layers, get, state, coef, gain, force):
     strips = state.shape[3]
     index = lax.broadcasted_iota(jnp.int32, (strips, WIN), 0)
     not_top = jnp.where(index == strips - 1, 0.0, 1.0)
@@ -178,95 +152,373 @@
             coef[f, 8, a] = g * (rx * vs + cx * vw) * low
             gain[f, a] = g
             force[f, a] = g * get(4 + f, a)
-    run_sweeps(state, coef, force)
+
+
+MESH = pl.DeviceIdType.MESH
+EARLY = 16
+
+
+def exchange(axis, peers, source, target, send_sem, recv_sem):
+    copies = []
+    for k, peer in enumerate(peers):
+        copy = pltpu.make_async_remote_copy(
+            src_ref=source(k, peer),
+            dst_ref=target(k),
+            send_sem=send_sem.at[k],
+            recv_sem=recv_sem.at[k],
+            device_id={axis: peer},
+            device_id_type=MESH,
+        )
+        copy.start()
+        copies.append(copy)
+    return copies
+
+
+def finish(copies):
+    for copy in copies:
+        copy.wait()
+
+
+def cut_window(tiles, own, t):
+    at = OFF + own * t
+    first, skip = at // LANES, at % LANES
+    if skip == 0:
+        return jnp.concatenate([tiles[first], tiles[first + 1]], axis=1)
+    keep = lax.broadcasted_iota(jnp.int32, (8, LANES), 1) < LANES - skip
+    turned = [pltpu.roll(tiles[first + j], LANES - skip, 1) for j in range(3)]
+    return jnp.concatenate(
+        [jnp.where(keep, turned[j], turned[j + 1]) for j in range(2)], axis=1
+    )
+
+
+def join_pieces(pieces, own, q):
+    lane = lax.broadcasted_iota(jnp.int32, (8, LANES), 1)
+    tile = None
+    for s, piece in enumerate(pieces):
+        shift = own * s - LANES * q
+        if shift + own <= 0 or shift >= LANES:
+            continue
+        moved = piece if shift % LANES == 0 else pltpu.roll(piece, shift % LANES, 1)
+        tile = moved if tile is None else jnp.where(lane >= shift, moved, tile)
+    return tile
+
+
+def fused_kernel(
+    strips,
+    parts,
+    guess_ref,
+    hard_ref,
+    thick_ref,
+    fric_ref,
+    ground_ref,
+    mask_ref,
+    drive_ref,
+    cell_ref,
+    east_ref,
+    north_ref,
+    weight_ref,
+    count_ref,
+    vel_ref,
+    grad_ref,
+    obs_out,
+    obs_in,
+    hard_buf,
+    hard_in,
+    maps_buf,
+    maps_in,
+    acc_ref,
+    send_a,
+    recv_a,
+    send_b,
+    recv_b,
+    send_c,
+    recv_c,
+    x_ref,
+    state,
+    coef,
+    gain,
+    force,
+    vel_out,
+    vel_in,
+    vel_all,
+    grad_out,
+    grad_in,
+    grad_all,
+    tile_send,
+    tile_recv,
+    layer_send,
+    layer_recv,
+):
+    cols = thick_ref.shape[1]
+    group = cols // parts
+    own = group // strips
+    step = group // LANES
+    span = hard_in.shape[1]
+    layers = float(hard_ref.shape[0] * parts)
+    me, layer = lax.axis_index("tile"), lax.axis_index("layer")
+    others = [lax.rem(me + k, strips) for k in range(1, strips)]
+    mates = [lax.rem(layer + k, parts) for k in range(1, parts)]
+
+    barrier = pltpu.get_barrier_semaphore()
+    for peer in others:
+        pl.semaphore_signal(barrier, inc=1, device_id={"tile": peer}, device_id_type=MESH)
+    for peer in mates:
+        pl.semaphore_signal(barrier, inc=1, device_id={"layer": peer}, device_id_type=MESH)
+
+    zero = jnp.zeros((8, LANES), jnp.float32)
+    total = hard_buf.shape[0]
+    for i in range(total):
+        at = (i - 1) * LANES
+        if 0 <= at < cols:
+            value = hard_ref[0, :, at : at + LANES]
+            for k in range(1, hard_ref.shape[0]):
+                value = value + hard_ref[k, :, at : at + LANES]
+            hard_buf[i] = value * thick_ref[:, at : at + LANES]
+        else:
+            hard_buf[i] = zero
+            for f in range(3):
+                maps_buf[f, i] = zero
+    slot = lax.broadcasted_iota(jnp.int32, (1, cell_ref.shape[3]), 1)
+    for d in range(strips):
+        obs_out[d, 0:1] = cell_ref[0, 0, d : d + 1].astype(jnp.float32)
+        obs_out[d, 1:2] = east_ref[0, 0, d : d + 1]
+        obs_out[d, 2:3] = north_ref[0, 0, d : d + 1]
+        obs_out[d, 3:4] = jnp.where(slot < count_ref[0, 0, d], weight_ref[0, 0, d : d + 1], 0.0)
+
+    def group_tiles(load):
+        tiles = []
+        for i in range(span):
+            at = group * layer + (i - 1) * LANES
+            if 1 <= i <= step:
+                tiles.append(load(pl.ds(pl.multiple_of(at, LANES), LANES)))
+            else:
+                inside = jnp.logical_and(at >= 0, at < cols)
+                safe = jnp.where(inside, at, 0)
+                value = load(pl.ds(pl.multiple_of(safe, LANES), LANES))
+                tiles.append(jnp.where(inside, value, 0.0))
+        return tiles
+
+    loads = [
+        lambda at: guess_ref[0, :, at],
+        lambda at: guess_ref[1, :, at],
+        lambda at: fric_ref[:, at] * ground_ref[:, at].astype(jnp.float32),
+        lambda at: mask_ref[:, at].astype(jnp.float32),
+        lambda at: drive_ref[0, :, at],
+        lambda at: drive_ref[1, :, at],
+    ]
+    for f, load in enumerate(loads):
+        tiles = group_tiles(load)
+        for t in range(strips):
+            send_a[t, f] = cut_window(tiles, own, t)
+
+    def tile_exchange(n, out, into):
+        return exchange(
+            "tile",
+            others,
+            lambda k, peer: out.at[peer],
+            lambda k: into.at[me],
+            tile_send.at[n],
+            tile_recv.at[n],
+        )
+
+    pl.semaphore_wait(barrier, strips + parts - 2)
+    hard_copies = exchange(
+        "layer",
+        mates,
+        lambda k, peer: hard_buf.at[pl.ds(step * peer, span)],
+        lambda k: hard_in.at[k],
+        layer_send.at[0],
+        layer_recv.at[0],
+    )
+    obs_copies = tile_exchange(0, obs_out, obs_in)
+    a_copies = tile_exchange(1, send_a, recv_a)
+    obs_in[me] = obs_out[me]
+    recv_a[me] = send_a[me]
+
+    finish(hard_copies)
+    tiles = []
+    for i in range(span):
+        value = hard_buf[step * layer + i]
+        for k in range(parts - 1):
+            value = value + hard_in[k, i]
+        tiles.append(value)
+    for t in range(strips):
+        send_b[t] = cut_window(tiles, own, t)
+    b_copies = tile_exchange(2, send_b, recv_b)
+    recv_b[me] = send_b[me]
+
+    finish(obs_copies)
+    for s in range(strips):
+        scatter_maps(
+            obs_in[s, 0:1].astype(jnp.int32),
+            obs_in[s, 1:2],
+            obs_in[s, 2:3],
+            obs_in[s, 3:4],
+            acc_ref,
+            cols,
+            s == 0,
+        )
+    n = 8 * (cols // WIN)
+    for f in range(3):
+        for i in range(cols // LANES):
+            at = 3 * f * n + 8 * (i // 2)
+            half = slice((i % 2) * LANES, (i % 2 + 1) * LANES)
+            maps_buf[f, i + 1] = (
+                acc_ref[at : at + 8, half]
+                + acc_ref[at + n : at + n + 8, half]
+                + acc_ref[at + 2 * n : at + 2 * n + 8, half]
+            )
+    maps_copies = exchange(
+        "layer",
+        mates,
+        lambda k, peer: maps_buf.at[:, pl.ds(step * peer, span)],
+        lambda k: maps_in.at[k],
+        layer_send.at[1],
+        layer_recv.at[1],
+    )
+
+    finish(a_copies)
+    finish(b_copies)
+    for f in range(6):
+        x_ref[f] = jnp.swapaxes(recv_a[:, f], 0, 1)
+    x_ref[6] = jnp.swapaxes(recv_b[...], 0, 1)
+
+    def get(f, a):
+        return x_ref[f, a]
+
+    make_coefs(layers, get, state, coef, gain, force)
+    run_sweeps(state, coef, force, EARLY)
+
+    finish(maps_copies)
+    for f in range(3):
+        tiles = []
+        for i in range(span):
+            value = maps_buf[f, step * layer + i]
+            for k in range(parts - 1):
+                value = value + maps_in[k, f, i]
+            tiles.append(value)
+        for t in range(strips):
+            send_c[t, f] = cut_window(tiles, own, t)
+    c_copies = tile_exchange(3, send_c, recv_c)
+    recv_c[me] = send_c[me]
+    run_sweeps(state, coef, force, SWEEPS - EARLY)
+
+    def own_part(value):
+        return pltpu.roll(value, WIN - HALO, 1)[:, :LANES]
+
+    for f in range(2):
+        parts_f = jnp.stack([own_part(state[0, f, a]) for a in range(8)], 0)
+        vel_out[:, f] = jnp.swapaxes(parts_f, 0, 1)
+    vel_copies = tile_exchange(4, vel_out, vel_in)
+    vel_in[me] = vel_out[me]
+
+    finish(c_copies)
+    for f in range(3):
+        x_ref[7 + f] = jnp.swapaxes(recv_c[:, f], 0, 1)
     for a in range(8):
         for f in range(2):
             vel = state[0, f, a]
-            put(f, a, vel)
             force[f, a] = gain[f, a] * (vel * get(7, a) - get(8 + f, a))
             gain[f, a] = vel
             state[0, f, a] = jnp.zeros_like(vel)
-    run_sweeps(state, coef, force)
-    for a in range(8):
-        put(2, a, -(get(2, a) * (gain[0, a] * state[0, 0, a] + gain[1, a] * state[0, 1, a])))
-
-
-def solve_call(layers, x_ref, out_ref, state, coef, gain, force):
-    def get(f, a):
-        return x_ref[f, a]
-
-    def put(f, a, value):
-        out_ref[f, a] = pltpu.roll(value, WIN - HALO, 1)[:, :LANES]
-
-    solve_kernel(layers, get, put, state, coef, gain, force)
-
-
-def on_device(
-    velocity_guess,
-    hardness,
-    thickness,
-    friction,
-    grounded,
-    ice_mask,
-    driving,
-    obs_cell,
-    obs_east,
-    obs_north,
-    obs_weight,
-    obs_count,
-):
+    run_sweeps(state, coef, force, EARLY)
+
+    def layer_gather(n, every):
+        here = every.at[:, pl.ds(step * layer, step)]
+        return exchange(
+            "layer", mates, lambda k, peer: here, lambda k: here, layer_send.at[n], layer_recv.at[n]
+        )
+
+    finish(vel_copies)
+    for f in range(2):
+        pieces = [vel_in[s, f] for s in range(strips)]
+        for q in range(step):
+            vel_all[f, step * layer + q] = join_pieces(pieces, own, q)
+    gather_copies = layer_gather(2, vel_all)
+    run_sweeps(state, coef, force, SWEEPS - EARLY)
+
+    rows = jnp.stack(
+        [
+            own_part(
+                -(get(2, a) * (gain[0, a] * state[0, 0, a] + gain[1, a] * state[0, 1, a]))
+            )
+            for a in range(8)
+        ],
+        0,
+    )
+    grad_out[...] = jnp.swapaxes(rows, 0, 1)
+    grad_copies = tile_exchange(5, grad_out, grad_in)
+    grad_in[me] = grad_out[me]
+    finish(gather_copies)
+    for f in range(2):
+        for i in range(cols // LANES):
+            vel_ref[f, :, i * LANES : (i + 1) * LANES] = vel_all[f, i]
+    finish(grad_copies)
+    pieces = [grad_in[s] for s in range(strips)]
+    for q in range(step):
+        grad_all[0, step * layer + q] = join_pieces(pieces, own, q)
+    finish(layer_gather(3, grad_all))
+    for i in range(cols // LANES):
+        grad_ref[:, i * LANES : (i + 1) * LANES] = grad_all[0, i]
+
+
+def on_device(*fields):
     strips, parts = lax.axis_size("tile"), lax.axis_size("layer")
-    cols = thickness.shape[1]
+    cols = fields[2].shape[1]
+    slots = fields[7].shape[3]
     group = cols // parts
     own = group // strips
-    span = -(-(OFF + own * (strips - 1) + WIN) // LANES) * LANES
-    layer = lax.axis_index("layer")
-    drag = friction * grounded.astype(jnp.float32)
-    inside = ice_mask.astype(jnp.float32)
-    valid = (lax.broadcasted_iota(jnp.int32, obs_weight.shape, 3) < obs_count[..., None]).astype(
-        jnp.float32
-    )
-    packed = jnp.stack(
-        [obs_cell.astype(jnp.float32), obs_east, obs_north, obs_weight * valid], 0
-    )[:, 0, 0]
-    arrived = lax.all_to_all(packed.swapaxes(0, 1), "tile", split_axis=0, concat_axis=0, tiled=True)
-    maps = pl.pallas_call(
-        maps_kernel,
-        out_shape=jax.ShapeDtypeStruct((4, 8, cols), jnp.float32),
-        scratch_shapes=[pltpu.VMEM((9 * 8 * (cols // WIN), WIN), jnp.float32)],
-        compiler_params=pltpu.CompilerParams(vmem_limit_bytes=VMEM_LIMIT),
-    )(arrived, hardness, thickness)
-    right = (parts - 1) * group + span - LANES - cols
-
-    def pad(x):
-        return jnp.pad(x, ((0, 0), (0, 0), (LANES, right)))
-
-    def windows(x):
-        return jnp.stack([x[:, :, OFF + own * t : OFF + own * t + WIN] for t in range(strips)], 0)
-
-    maps = pad(maps)
-    shares = jnp.stack([maps[:, :, group * p : group * p + span] for p in range(parts)], 0)
-    summed = lax.psum_scatter(shares, "layer", scatter_dimension=0, tiled=False)
-    plain = pad(jnp.concatenate([velocity_guess, drag[None], inside[None], driving], 0))
-    plain = lax.dynamic_slice_in_dim(plain, layer * group, span, axis=2)
-    send = windows(jnp.concatenate([plain, summed], 0))
-    got = lax.all_to_all(send, "tile", split_axis=0, concat_axis=0, tiled=True)
-    block = got.transpose(1, 2, 0, 3)
-    result = pl.pallas_call(
-        functools.partial(solve_call, float(hardness.shape[0] * parts)),
-        out_shape=jax.ShapeDtypeStruct((3, 8, strips, LANES), jnp.float32),
+    span = -(-(OFF + own * (strips - 1) + WIN) // LANES)
+    total = group // LANES * (parts - 1) + span
+    tiles = cols // LANES
+
+    def vmem(*shape):
+        return pltpu.VMEM(shape, jnp.float32)
+
+    in_specs = [pl.BlockSpec(memory_space=pltpu.VMEM)] * 11
+    in_specs.append(pl.BlockSpec(memory_space=pltpu.SMEM))
+    return pl.pallas_call(
+        functools.partial(fused_kernel, strips, parts),
+        out_shape=(
+            jax.ShapeDtypeStruct((2, 8, cols), jnp.float32),
+            jax.ShapeDtypeStruct((8, cols), jnp.float32),
+        ),
+        in_specs=in_specs,
+        out_specs=(pl.BlockSpec(memory_space=pltpu.VMEM),) * 2,
         scratch_shapes=[
-            pltpu.VMEM((2, 2, 8, strips, WIN), jnp.float32),
-            pltpu.VMEM((2, 9, 8, strips, WIN), jnp.float32),
-            pltpu.VMEM((2, 8, strips, WIN), jnp.float32),
-            pltpu.VMEM((2, 8, strips, WIN), jnp.float32),
+            vmem(strips, 4, slots),
+            vmem(strips, 4, slots),
+            vmem(total, 8, LANES),
+            vmem(parts - 1, span, 8, LANES),
+            vmem(3, total, 8, LANES),
+            vmem(parts - 1, 3, span, 8, LANES),
+            vmem(9 * 8 * (cols // WIN), WIN),
+            vmem(strips, 6, 8, WIN),
+            vmem(strips, 6, 8, WIN),
+            vmem(strips, 8, WIN),
+            vmem(strips, 8, WIN),
+            vmem(strips, 3, 8, WIN),
+            vmem(strips, 3, 8, WIN),
+            vmem(10, 8, strips, WIN),
+            vmem(2, 2, 8, strips, WIN),
+            vmem(2, 9, 8, strips, WIN),
+            vmem(2, 8, strips, WIN),
+            vmem(2, 8, strips, WIN),
+            vmem(strips, 2, 8, LANES),
+            vmem(strips, 2, 8, LANES),
+            vmem(2, tiles, 8, LANES),
+            vmem(strips, 8, LANES),
+            vmem(strips, 8, LANES),
+            vmem(1, tiles, 8, LANES),
+            pltpu.SemaphoreType.DMA((6, strips - 1)),
+            pltpu.SemaphoreType.DMA((6, strips - 1)),
+            pltpu.SemaphoreType.DMA((4, parts - 1)),
+            pltpu.SemaphoreType.DMA((4, parts - 1)),
         ],
-        compiler_params=pltpu.CompilerParams(vmem_limit_bytes=VMEM_LIMIT),
-    )(block)
-    back = lax.all_to_all(result.transpose(2, 0, 1, 3), "tile", split_axis=0, concat_axis=0, tiled=True)
-    mine = back[..., :own].transpose(1, 2, 0, 3).reshape(3, 8, group)
-    full = lax.all_gather(mine, "layer", axis=2, tiled=True)
-    return full[:2], full[2]
+        compiler_params=pltpu.CompilerParams(
+            collective_id=0, has_side_effects=True, vmem_limit_bytes=VMEM_LIMIT
+        ),
+    )(*fields)
 
 
 def solution(mesh):

time: 110 us -> 56 us (0.51)
  blocking collectives: 53 us -> 0 us
  Pallas kernels: 15 us -> 43.5 us
  waiting for transfers between devices: 17.4 us -> 0 us
  between operations: 14.2 us -> 0.66 us
  local copies, waits for them, and re-layouts: 5.41 us -> 11.3 us
  other arithmetic: 4.05 us -> 0 us
    all_to_all x3 -> x0, blocking collectives: 47.2 us -> none  [the longest x1 23 us: on_device(): got = lax.all_to_all(send, 'tile', split_axis=0, concat_axis=0, tiled=True)]
    pallas_call x2 -> x1, Pallas kernels: 15 us -> 43.5 us  [on_device(): pl.pallas_call(functools.partial(fused_kernel, strips, parts), out_shape=...]
    reduce_scatter x1 -> x0, waiting for transfers between devices: 17.4 us -> none  [on_device(): summed = lax.psum_scatter(shares, 'layer', scatter_dimension=0, tiled=False)]
    unnamed x18 -> x26, local copies, waits for them, and re-layouts: 2.77 us -> 11.3 us
    all_gather x1 -> x0, blocking collectives: 5.88 us -> none  [on_device(): full = lax.all_gather(mine, 'layer', axis=2, tiled=True)]
    another operation x3 -> x0, other arithmetic: 1.71 us -> none  [the longest x1 0.83 us: on_device(): jnp.stack([maps[:, :, group * p:group * p + span] for p in range(parts)], 0)]
    unnamed x7 -> x0, other arithmetic: 1.45 us -> none
  transfers between devices with their start and end apart: 1 -> 0, of which waited for: 1 -> 0; matrix products, arithmetic and copies ran while one was open for 0% -> 0% of each run, Pallas kernels for 0% -> 0%
where the time goes in v2:
time: 56 us; the launch traced here: 55.5 us
  Pallas kernels  43.5 us (78%)
  local copies, waits for them, and re-layouts  11.3 us (20%)
  between operations  0.66 us (1%)
    pallas_call x1, Pallas kernels, on_device(): pl.pallas_call(functools.partial(fused_kernel, strips, parts), out_shape=...  43.5 us
    unnamed x26, local copies, waits for them, and re-layouts  11.3 us

profile of v2, /device:TPU:0, one launch (start us, length us, event | category | flops | bytes accessed | tf_op | source)
XLA Modules:
  0.0 55.5 jit_solution(14472994611066088820)
XLA Ops:
  0.6 0.0 copy-start
  0.6 1.0 %copy-done = f32[4,8,3072]{2,1,0:T(8,128)S(1)} copy-done((f32[4,8,3072]{2,1,0:T(8,128)S(1)}, f32[4,8,3072]{2,1,0:T(8,128)}, u32[]{:S(2)}) %copy-start) | copy-done | bytes 393240
  1.6 0.0 copy-start.1
  1.6 0.9 %copy-done.1 = f32[2,8,3072]{2,1,0:T(8,128)S(1)} copy-done((f32[2,8,3072]{2,1,0:T(8,128)S(1)}, f32[2,8,3072]{2,1,0:T(8,128)}, u32[]{:S(2)}) %copy-start.1) | copy-done | bytes 196632
  2.6 0.0 copy-start.2
  2.6 0.9 %copy-done.2 = f32[2,8,3072]{2,1,0:T(8,128)S(1)} copy-done((f32[2,8,3072]{2,1,0:T(8,128)S(1)}, f32[2,8,3072]{2,1,0:T(8,128)}, u32[]{:S(2)}) %copy-start.2) | copy-done | bytes 196632
  3.5 0.0 copy-start.3
  3.5 0.9 %copy-done.3 = f32[8,3072]{1,0:T(8,128)S(1)} copy-done((f32[8,3072]{1,0:T(8,128)S(1)}, f32[8,3072]{1,0:T(8,128)}, u32[]{:S(2)}) %copy-start.3) | copy-done | bytes 98328
  4.4 0.0 copy-start.4
  4.4 0.9 %copy-done.4 = f32[8,3072]{1,0:T(8,128)S(1)} copy-done((f32[8,3072]{1,0:T(8,128)S(1)}, f32[8,3072]{1,0:T(8,128)}, u32[]{:S(2)}) %copy-start.4) | copy-done | bytes 98328
  5.3 0.0 copy-start.5
  5.3 0.9 %copy-done.5 = s32[8,3072]{1,0:T(8,128)S(1)} copy-done((s32[8,3072]{1,0:T(8,128)S(1)}, s32[8,3072]{1,0:T(8,128)}, u32[]{:S(2)}) %copy-start.5) | copy-done | bytes 98328
  6.2 0.0 copy-start.6
  6.2 0.9 %copy-done.6 = s32[8,3072]{1,0:T(8,128)S(1)} copy-done((s32[8,3072]{1,0:T(8,128)S(1)}, s32[8,3072]{1,0:T(8,128)}, u32[]{:S(2)}) %copy-start.6) | copy-done | bytes 98328
  7.1 0.0 copy-start.7
  7.1 0.7 %copy-done.7 = s32[1,1,8,512]{3,2,1,0:T(8,128)S(1)} copy-done((s32[1,1,8,512]{3,2,1,0:T(8,128)S(1)}, s32[1,1,8,512]{3,2,1,0:T(8,128)}, u32[]{:S(2)}) %copy-start.7) | copy-done | bytes 16408
  7.8 0.0 copy-start.8
  7.8 0.7 %copy-done.8 = f32[1,1,8,512]{3,2,1,0:T(8,128)S(1)} copy-done((f32[1,1,8,512]{3,2,1,0:T(8,128)S(1)}, f32[1,1,8,512]{3,2,1,0:T(8,128)}, u32[]{:S(2)}) %copy-start.8) | copy-done | bytes 16408
  8.5 0.7 %copy-done.9 = f32[1,1,8,512]{3,2,1,0:T(8,128)S(1)} copy-done((f32[1,1,8,512]{3,2,1,0:T(8,128)S(1)}, f32[1,1,8,512]{3,2,1,0:T(8,128)}, u32[]{:S(2)}) %copy-start.9) | copy-done | bytes 16408
  9.2 0.7 %copy-done.10 = f32[1,1,8,512]{3,2,1,0:T(8,128)S(1)} copy-done((f32[1,1,8,512]{3,2,1,0:T(8,128)S(1)}, f32[1,1,8,512]{3,2,1,0:T(8,128)}, u32[]{:S(2)}) %copy-start.10) | copy-done | bytes 16408
  9.9 0.7 %copy-done.11 = s32[1,1,8]{2,1,0:T(1,128)S(1)} copy-done((s32[1,1,8]{2,1,0:T(1,128)S(1)}, s32[1,1,8]{2,1,0:T(1,128)}, u32[]{:S(2)}) %copy-start.11) | copy-done | bytes 56
  10.6 43.5 %shard_map.131 = (f32[2,8,3072]{2,1,0:T(8,128)S(1)}, f32[8,3072]{1,0:T(8,128)S(1)}) custom-call(f32[2,8,3072]{2,1,0:T(8,128)S(1)} %copy-done.1, f32[4,8,3072]{2,1,0:T(8,128)S(1)} %copy-done, f32[8,3072]{1,0:T(8,128)S(1)} %copy-done.3, f32[8,3072]{1,0:T(8,128)S(1)} %copy-done.4, s32[8,3072]{1,0:T(8,128)S(1)} %copy-done.5, s32[8,3072]{1,0:T(8,128)S(1)} %copy-done.6, ...), custom_call_target="tpu_custom_call" | custom-call | tf_op jit(solution)/shard_map/pallas_call | solution.py:480
  54.1 0.7 %copy.16 = f32[2,8,3072]{2,1,0:T(8,128)} copy(f32[2,8,3072]{2,1,0:T(8,128)S(1)} %get-tuple-element.4) | data formatting | bytes 393216
  54.8 0.6 %copy.17 = f32[8,3072]{1,0:T(8,128)} copy(f32[8,3072]{1,0:T(8,128)S(1)} %get-tuple-element.5) | data formatting | bytes 196608
  (3 shorter events, 0.0 us)
Async XLA Ops:
  0.6 1.0 %copy-start = (f32[4,8,3072]{2,1,0:T(8,128)S(1)}, f32[4,8,3072]{2,1,0:T(8,128)}, u32[]{:S(2)}) copy-start(f32[4,8,3072]{2,1,0:T(8,128)} %hard_ref.1) | copy-start | bytes 1179652
  1.6 0.9 %copy-start.1 = (f32[2,8,3072]{2,1,0:T(8,128)S(1)}, f32[2,8,3072]{2,1,0:T(8,128)}, u32[]{:S(2)}) copy-start(f32[2,8,3072]{2,1,0:T(8,128)} %guess_ref.1) | copy-start | bytes 589828
  2.6 0.9 %copy-start.2 = (f32[2,8,3072]{2,1,0:T(8,128)S(1)}, f32[2,8,3072]{2,1,0:T(8,128)}, u32[]{:S(2)}) copy-start(f32[2,8,3072]{2,1,0:T(8,128)} %drive_ref.1) | copy-start | bytes 589828
  3.5 0.9 %copy-start.3 = (f32[8,3072]{1,0:T(8,128)S(1)}, f32[8,3072]{1,0:T(8,128)}, u32[]{:S(2)}) copy-start(f32[8,3072]{1,0:T(8,128)} %thick_ref.1) | copy-start | bytes 294916
  4.4 0.9 %copy-start.4 = (f32[8,3072]{1,0:T(8,128)S(1)}, f32[8,3072]{1,0:T(8,128)}, u32[]{:S(2)}) copy-start(f32[8,3072]{1,0:T(8,128)} %fric_ref.1) | copy-start | bytes 294916
  5.3 0.9 %copy-start.5 = (s32[8,3072]{1,0:T(8,128)S(1)}, s32[8,3072]{1,0:T(8,128)}, u32[]{:S(2)}) copy-start(s32[8,3072]{1,0:T(8,128)} %ground_ref.1) | copy-start | bytes 294916
  6.2 0.9 %copy-start.6 = (s32[8,3072]{1,0:T(8,128)S(1)}, s32[8,3072]{1,0:T(8,128)}, u32[]{:S(2)}) copy-start(s32[8,3072]{1,0:T(8,128)} %mask_ref.1) | copy-start | bytes 294916
  7.1 0.7 %copy-start.7 = (s32[1,1,8,512]{3,2,1,0:T(8,128)S(1)}, s32[1,1,8,512]{3,2,1,0:T(8,128)}, u32[]{:S(2)}) copy-start(s32[1,1,8,512]{3,2,1,0:T(8,128)} %cell_ref.1) | copy-start | bytes 49156
  7.8 0.7 %copy-start.8 = (f32[1,1,8,512]{3,2,1,0:T(8,128)S(1)}, f32[1,1,8,512]{3,2,1,0:T(8,128)}, u32[]{:S(2)}) copy-start(f32[1,1,8,512]{3,2,1,0:T(8,128)} %east_ref.1) | copy-start | bytes 49156
  8.5 0.7 %copy-start.9 = (f32[1,1,8,512]{3,2,1,0:T(8,128)S(1)}, f32[1,1,8,512]{3,2,1,0:T(8,128)}, u32[]{:S(2)}) copy-start(f32[1,1,8,512]{3,2,1,0:T(8,128)} %north_ref.1) | copy-start | bytes 49156
  9.2 0.7 %copy-start.10 = (f32[1,1,8,512]{3,2,1,0:T(8,128)S(1)}, f32[1,1,8,512]{3,2,1,0:T(8,128)}, u32[]{:S(2)}) copy-start(f32[1,1,8,512]{3,2,1,0:T(8,128)} %weight_ref.1) | copy-start | bytes 49156
  9.9 0.7 %copy-start.11 = (s32[1,1,8]{2,1,0:T(1,128)S(1)}, s32[1,1,8]{2,1,0:T(1,128)}, u32[]{:S(2)}) copy-start(s32[1,1,8]{2,1,0:T(1,128)} %count_ref.1) | copy-start | bytes 100

commit v3 on v2

--- a/solution.py
+++ b/solution.py
@@ -14,7 +14,7 @@
 WIN = 256
 LANES = 128
 OFF = LANES - HALO
-VMEM_LIMIT = 48 * 1024 * 1024
+VMEM_LIMIT = 60 * 1024 * 1024
 
 
 def scatter_maps(cell, east, north, weight, acc_ref, cols, first):
@@ -155,7 +155,8 @@
 
 
 MESH = pl.DeviceIdType.MESH
-EARLY = 16
+EARLY = 4
+RETURN = 16
 
 
 def exchange(axis, peers, source, target, send_sem, recv_sem):
@@ -206,20 +207,10 @@
 def fused_kernel(
     strips,
     parts,
-    guess_ref,
-    hard_ref,
-    thick_ref,
-    fric_ref,
-    ground_ref,
-    mask_ref,
-    drive_ref,
-    cell_ref,
-    east_ref,
-    north_ref,
-    weight_ref,
-    count_ref,
-    vel_ref,
-    grad_ref,
+    *refs,
+):
+    args, (vel_ref, grad_ref), held = refs[:12], refs[12:14], refs[14:26]
+    (
     obs_out,
     obs_in,
     hard_buf,
@@ -248,7 +239,22 @@
     tile_recv,
     layer_send,
     layer_recv,
-):
+    load_sem,
+    ) = refs[26:]
+    (
+        guess_ref,
+        hard_ref,
+        thick_ref,
+        fric_ref,
+        ground_ref,
+        mask_ref,
+        drive_ref,
+        cell_ref,
+        east_ref,
+        north_ref,
+        weight_ref,
+        count_ref,
+    ) = held
     cols = thick_ref.shape[1]
     group = cols // parts
     own = group // strips
@@ -265,6 +271,14 @@
     for peer in mates:
         pl.semaphore_signal(barrier, inc=1, device_id={"layer": peer}, device_id_type=MESH)
 
+    arrivals = [
+        pltpu.make_async_copy(args[n], held[n], load_sem.at[n]) for n in range(len(args))
+    ]
+    for n in (7, 8, 9, 10, 11, 1, 2, 0, 3, 4, 5, 6):
+        arrivals[n].start()
+
+    for n in (1, 2):
+        arrivals[n].wait()
     zero = jnp.zeros((8, LANES), jnp.float32)
     total = hard_buf.shape[0]
     for i in range(total):
@@ -278,13 +292,17 @@
             hard_buf[i] = zero
             for f in range(3):
                 maps_buf[f, i] = zero
+    for n in (7, 8, 9, 10, 11):
+        arrivals[n].wait()
     slot = lax.broadcasted_iota(jnp.int32, (1, cell_ref.shape[3]), 1)
     for d in range(strips):
         obs_out[d, 0:1] = cell_ref[0, 0, d : d + 1].astype(jnp.float32)
         obs_out[d, 1:2] = east_ref[0, 0, d : d + 1]
         obs_out[d, 2:3] = north_ref[0, 0, d : d + 1]
-        obs_out[d, 3:4] = jnp.where(slot < count_ref[0, 0, d], weight_ref[0, 0, d : d + 1], 0.0)
-
+        obs_out[d, 3:4] = jnp.where(slot < count_ref[0, :, d : d + 1], weight_ref[0, 0, d : d + 1], 0.0)
+
+    for n in (0, 3, 4, 5, 6):
+        arrivals[n].wait()
     def group_tiles(load):
         tiles = []
         for i in range(span):
@@ -421,7 +439,7 @@
             force[f, a] = gain[f, a] * (vel * get(7, a) - get(8 + f, a))
             gain[f, a] = vel
             state[0, f, a] = jnp.zeros_like(vel)
-    run_sweeps(state, coef, force, EARLY)
+    run_sweeps(state, coef, force, RETURN)
 
     def layer_gather(n, every):
         here = every.at[:, pl.ds(step * layer, step)]
@@ -435,7 +453,7 @@
         for q in range(step):
             vel_all[f, step * layer + q] = join_pieces(pieces, own, q)
     gather_copies = layer_gather(2, vel_all)
-    run_sweeps(state, coef, force, SWEEPS - EARLY)
+    run_sweeps(state, coef, force, SWEEPS - RETURN)
 
     rows = jnp.stack(
         [
@@ -475,17 +493,16 @@
     def vmem(*shape):
         return pltpu.VMEM(shape, jnp.float32)
 
-    in_specs = [pl.BlockSpec(memory_space=pltpu.VMEM)] * 11
-    in_specs.append(pl.BlockSpec(memory_space=pltpu.SMEM))
     return pl.pallas_call(
         functools.partial(fused_kernel, strips, parts),
         out_shape=(
             jax.ShapeDtypeStruct((2, 8, cols), jnp.float32),
             jax.ShapeDtypeStruct((8, cols), jnp.float32),
         ),
-        in_specs=in_specs,
+        in_specs=[pl.BlockSpec(memory_space=pl.ANY)] * len(fields),
         out_specs=(pl.BlockSpec(memory_space=pltpu.VMEM),) * 2,
-        scratch_shapes=[
+        scratch_shapes=[pltpu.VMEM(x.shape, x.dtype) for x in fields]
+        + [
             vmem(strips, 4, slots),
             vmem(strips, 4, slots),
             vmem(total, 8, LANES),
@@ -514,6 +531,7 @@
             pltpu.SemaphoreType.DMA((6, strips - 1)),
             pltpu.SemaphoreType.DMA((4, parts - 1)),
             pltpu.SemaphoreType.DMA((4, parts - 1)),
+            pltpu.SemaphoreType.DMA((len(fields),)),
         ],
         compiler_params=pltpu.CompilerParams(
             collective_id=0, has_side_effects=True, vmem_limit_bytes=VMEM_LIMIT

time: 56 us -> 45.7 us (0.82)
  local copies, waits for them, and re-layouts: 11.3 us -> 2.3 us
  Pallas kernels: 43.5 us -> 42.6 us
    unnamed x26 -> x4, local copies, waits for them, and re-layouts: 11.3 us -> 2.3 us
    pallas_call x1, Pallas kernels: 43.5 us -> 42.6 us  [on_device(): pl.pallas_call(functools.partial(fused_kernel, strips, parts), out_shape=...]
where the time goes in v3:
time: 45.7 us; the launch traced here: 45.5 us
  Pallas kernels  42.6 us (93%)
  local copies, waits for them, and re-layouts  2.3 us (5%)
  between operations  0.65 us (1%)
    pallas_call x1, Pallas kernels, on_device(): pl.pallas_call(functools.partial(fused_kernel, strips, parts), out_shape=...  42.6 us
    unnamed x4, local copies, waits for them, and re-layouts  2.3 us

profile of v3, /device:TPU:0, one launch (start us, length us, event | category | flops | bytes accessed | tf_op | source)
XLA Modules:
  0.0 45.5 jit_solution(1130945628939765245)
XLA Ops:
  0.6 42.6 %shard_map.131 = (f32[2,8,3072]{2,1,0:T(8,128)}, f32[8,3072]{1,0:T(8,128)}) custom-call(f32[2,8,3072]{2,1,0:T(8,128)} %refs_0_.1, f32[4,8,3072]{2,1,0:T(8,128)} %refs_1_.1, f32[8,3072]{1,0:T(8,128)} %refs_2_.1, f32[8,3072]{1,0:T(8,128)} %refs_3_.1, s32[8,3072]{1,0:T(8,128)} %refs_4_.1, s32[8,3072]{1,0:T(8,128)} %refs_5_.1, f32[2,8,3072]{2,1,0:T(8,128)} %refs_6_.1, ...), custom_call_target="tpu_custom_call" | custom-call | tf_op jit(solution)/shard_map/pallas_call | solution.py:496
  43.2 0.0 copy-start
  43.2 1.7 %copy.16 = f32[2,8,3072]{2,1,0:T(8,128)} copy(f32[2,8,3072]{2,1,0:T(8,128)} %get-tuple-element.4) | data formatting | bytes 393216
  44.9 0.0 copy-done
  44.9 0.6 %copy.17 = f32[8,3072]{1,0:T(8,128)} copy(f32[8,3072]{1,0:T(8,128)S(1)} %copy-done) | data formatting | bytes 196608
Async XLA Ops:
  43.2 1.7 %copy-start = (f32[8,3072]{1,0:T(8,128)S(1)}, f32[8,3072]{1,0:T(8,128)}, u32[]{:S(2)}) copy-start(f32[8,3072]{1,0:T(8,128)} %get-tuple-element.5) | copy-start | bytes 294916

commit v4 on v3

--- a/solution.py
+++ b/solution.py
@@ -10,22 +10,23 @@
 SWEEPS = 40
 OMEGA = 0.5
 REGULAR = 0.01
-HALO = 2 * SWEEPS
-WIN = 256
+HALO = 16
 LANES = 128
+WIN = LANES
+BLOCK = 2 * LANES
 OFF = LANES - HALO
 VMEM_LIMIT = 60 * 1024 * 1024
 
 
 def scatter_maps(cell, east, north, weight, acc_ref, cols, first):
-    blocks = cols // WIN
+    blocks = cols // BLOCK
     slots = cell.shape[1]
     row = jnp.zeros_like(cell)
     for r in range(1, 8):
         row = row + jnp.where(cell >= r * cols, 1, 0)
     rem = cell - row * cols
-    high = (rem // WIN) * 8 + row
-    low = rem % WIN
+    high = (rem // BLOCK) * 8 + row
+    low = rem % BLOCK
     hit = lax.broadcasted_iota(jnp.int32, (8 * blocks, slots), 0) == high
     terms = []
     for value in (weight, weight * east, weight * north):
@@ -36,7 +37,7 @@
             terms.append(jnp.where(hit, part, 0.0).astype(jnp.bfloat16))
     lhs = jnp.concatenate(terms, axis=0)
     rhs = jnp.where(
-        lax.broadcasted_iota(jnp.int32, (WIN, slots), 0) == low, 1.0, 0.0
+        lax.broadcasted_iota(jnp.int32, (BLOCK, slots), 0) == low, 1.0, 0.0
     ).astype(jnp.bfloat16)
     prod = lax.dot_general(
         lhs, rhs, (((1,), (1,)), ((), ())), preferred_element_type=jnp.float32
@@ -83,15 +84,11 @@
             for f in range(2):
                 g = 1 - f
                 c = lambda k: coef[f, k, a]
-                new = c(0) * here[f][0] + force[f, a]
-                new = new + c(1) * after[f][0]
-                new = new + c(2) * before[f][0]
-                new = new + c(3) * here[f][1]
-                new = new + c(4) * here[f][2]
-                new = new + c(5) * after[g][1]
-                new = new + c(6) * after[g][2]
-                new = new + c(7) * before[g][1]
-                new = new + c(8) * before[g][2]
+                near = c(0) * here[f][0] + force[f, a]
+                near = near + (c(3) * here[f][1] + c(4) * here[f][2])
+                over = c(1) * after[f][0] + (c(5) * after[g][1] + c(6) * after[g][2])
+                under = c(2) * before[f][0] + (c(7) * before[g][1] + c(8) * before[g][2])
+                new = near + (over + under)
                 state[dst, f, a] = new
             before, here = here, after
 
@@ -155,8 +152,7 @@
 
 
 MESH = pl.DeviceIdType.MESH
-EARLY = 4
-RETURN = 16
+LEGS = (14, 14, 12)
 
 
 def exchange(axis, peers, source, target, send_sem, recv_sem):
@@ -180,16 +176,31 @@
         copy.wait()
 
 
-def cut_window(tiles, own, t):
-    at = OFF + own * t
+def cut_window(tiles, own, pos):
+    at = OFF + own * pos
     first, skip = at // LANES, at % LANES
     if skip == 0:
-        return jnp.concatenate([tiles[first], tiles[first + 1]], axis=1)
+        return tiles[first]
     keep = lax.broadcasted_iota(jnp.int32, (8, LANES), 1) < LANES - skip
-    turned = [pltpu.roll(tiles[first + j], LANES - skip, 1) for j in range(3)]
-    return jnp.concatenate(
-        [jnp.where(keep, turned[j], turned[j + 1]) for j in range(2)], axis=1
-    )
+    turned = [pltpu.roll(tiles[first + j], LANES - skip, 1) for j in range(2)]
+    return jnp.where(keep, turned[0], turned[1])
+
+
+def snake(index, strips):
+    inner = max(1, strips // 4)
+    outer, rest = index // inner, index % inner
+    return outer * inner + rest + (outer % 2) * (inner - 1 - 2 * rest)
+
+
+def position(tile, layer, strips):
+    pos = snake(tile, strips)
+    return pos + (layer % 2) * (strips - 1 - 2 * pos)
+
+
+def device_at(place, strips, parts):
+    place = place % (strips * parts)
+    layer, pos = place // strips, place % strips
+    return snake(pos + (layer % 2) * (strips - 1 - 2 * pos), strips), layer
 
 
 def join_pieces(pieces, own, q):
@@ -240,6 +251,10 @@
     layer_send,
     layer_recv,
     load_sem,
+    halo_out,
+    halo_in,
+    halo_send,
+    halo_recv,
     ) = refs[26:]
     (
         guess_ref,
@@ -265,6 +280,10 @@
     others = [lax.rem(me + k, strips) for k in range(1, strips)]
     mates = [lax.rem(layer + k, parts) for k in range(1, parts)]
 
+    spot = position(me, layer, strips)
+    place = layer * strips + spot
+    sides = [device_at(place + strips * parts - 1, strips, parts), device_at(place + 1, strips, parts)]
+
     barrier = pltpu.get_barrier_semaphore()
     for peer in others:
         pl.semaphore_signal(barrier, inc=1, device_id={"tile": peer}, device_id_type=MESH)
@@ -329,12 +348,12 @@
         for t in range(strips):
             send_a[t, f] = cut_window(tiles, own, t)
 
-    def tile_exchange(n, out, into):
+    def tile_exchange(n, out, into, back=False, window=False):
         return exchange(
             "tile",
             others,
-            lambda k, peer: out.at[peer],
-            lambda k: into.at[me],
+            lambda k, peer: out.at[position(peer, layer, strips) if window else peer],
+            lambda k: into.at[spot if back else me],
             tile_send.at[n],
             tile_recv.at[n],
         )
@@ -349,9 +368,9 @@
         layer_recv.at[0],
     )
     obs_copies = tile_exchange(0, obs_out, obs_in)
-    a_copies = tile_exchange(1, send_a, recv_a)
+    a_copies = tile_exchange(1, send_a, recv_a, window=True)
     obs_in[me] = obs_out[me]
-    recv_a[me] = send_a[me]
+    recv_a[me] = send_a[spot]
 
     finish(hard_copies)
     tiles = []
@@ -362,8 +381,8 @@
         tiles.append(value)
     for t in range(strips):
         send_b[t] = cut_window(tiles, own, t)
-    b_copies = tile_exchange(2, send_b, recv_b)
-    recv_b[me] = send_b[me]
+    b_copies = tile_exchange(2, send_b, recv_b, window=True)
+    recv_b[me] = send_b[spot]
 
     finish(obs_copies)
     for s in range(strips):
@@ -376,7 +395,7 @@
             cols,
             s == 0,
         )
-    n = 8 * (cols // WIN)
+    n = 8 * (cols // BLOCK)
     for f in range(3):
         for i in range(cols // LANES):
             at = 3 * f * n + 8 * (i // 2)
@@ -405,8 +424,48 @@
         return x_ref[f, a]
 
     make_coefs(layers, get, state, coef, gain, force)
-    run_sweeps(state, coef, force, EARLY)
-
+    lane = lax.broadcasted_iota(jnp.int32, (strips, LANES), 1)
+
+    def send_halos(n):
+        for f in range(2):
+            left = right = None
+            for a in range(8):
+                value = state[0, f, a]
+                to_left = pltpu.roll(value, (HALO * a - HALO) % LANES, 1)
+                to_right = pltpu.roll(value, (HALO * a - own) % LANES, 1)
+                left = to_left if a == 0 else jnp.where(lane >= HALO * a, to_left, left)
+                right = to_right if a == 0 else jnp.where(lane >= HALO * a, to_right, right)
+            halo_out[n, 0, f] = left
+            halo_out[n, 1, f] = right
+        copies = []
+        for side, (tile, part) in enumerate(sides):
+            copy = pltpu.make_async_remote_copy(
+                src_ref=halo_out.at[n, side],
+                dst_ref=halo_in.at[n, side],
+                send_sem=halo_send.at[n, side],
+                recv_sem=halo_recv.at[n, side],
+                device_id={"tile": tile, "layer": part},
+                device_id_type=MESH,
+            )
+            copy.start()
+            copies.append(copy)
+        return copies
+
+    def take_halos(n, copies):
+        finish(copies)
+        low = lane < HALO
+        high = jnp.logical_and(lane >= HALO + own, lane < 2 * HALO + own)
+        for f in range(2):
+            from_left = jnp.where(place > 0, halo_in[n, 1, f], 0.0)
+            from_right = jnp.where(place < strips * parts - 1, halo_in[n, 0, f], 0.0)
+            for a in range(8):
+                west = pltpu.roll(from_left, (LANES - HALO * a) % LANES, 1)
+                east = pltpu.roll(from_right, (HALO + own - HALO * a) % LANES, 1)
+                value = jnp.where(low, west, state[0, f, a])
+                state[0, f, a] = jnp.where(high, east, value)
+
+    run_sweeps(state, coef, force, LEGS[0])
+    halos = send_halos(0)
     finish(maps_copies)
     for f in range(3):
         tiles = []
@@ -417,29 +476,33 @@
             tiles.append(value)
         for t in range(strips):
             send_c[t, f] = cut_window(tiles, own, t)
-    c_copies = tile_exchange(3, send_c, recv_c)
-    recv_c[me] = send_c[me]
-    run_sweeps(state, coef, force, SWEEPS - EARLY)
+    c_copies = tile_exchange(3, send_c, recv_c, window=True)
+    recv_c[me] = send_c[spot]
+    take_halos(0, halos)
+    run_sweeps(state, coef, force, LEGS[1])
+    take_halos(1, send_halos(1))
+    run_sweeps(state, coef, force, LEGS[2])
+    halos = send_halos(2)
 
     def own_part(value):
-        return pltpu.roll(value, WIN - HALO, 1)[:, :LANES]
+        return pltpu.roll(value, WIN - HALO, 1)
 
     for f in range(2):
         parts_f = jnp.stack([own_part(state[0, f, a]) for a in range(8)], 0)
         vel_out[:, f] = jnp.swapaxes(parts_f, 0, 1)
-    vel_copies = tile_exchange(4, vel_out, vel_in)
-    vel_in[me] = vel_out[me]
-
+    vel_copies = tile_exchange(4, vel_out, vel_in, back=True)
+    vel_in[spot] = vel_out[me]
     finish(c_copies)
     for f in range(3):
         x_ref[7 + f] = jnp.swapaxes(recv_c[:, f], 0, 1)
+    take_halos(2, halos)
     for a in range(8):
         for f in range(2):
             vel = state[0, f, a]
             force[f, a] = gain[f, a] * (vel * get(7, a) - get(8 + f, a))
             gain[f, a] = vel
             state[0, f, a] = jnp.zeros_like(vel)
-    run_sweeps(state, coef, force, RETURN)
+    run_sweeps(state, coef, force, LEGS[0])
 
     def layer_gather(n, every):
         here = every.at[:, pl.ds(step * layer, step)]
@@ -447,13 +510,17 @@
             "layer", mates, lambda k, peer: here, lambda k: here, layer_send.at[n], layer_recv.at[n]
         )
 
+    halos = send_halos(3)
     finish(vel_copies)
     for f in range(2):
         pieces = [vel_in[s, f] for s in range(strips)]
         for q in range(step):
             vel_all[f, step * layer + q] = join_pieces(pieces, own, q)
     gather_copies = layer_gather(2, vel_all)
-    run_sweeps(state, coef, force, SWEEPS - RETURN)
+    take_halos(3, halos)
+    run_sweeps(state, coef, force, LEGS[1])
+    take_halos(4, send_halos(4))
+    run_sweeps(state, coef, force, LEGS[2])
 
     rows = jnp.stack(
         [
@@ -465,8 +532,8 @@
         0,
     )
     grad_out[...] = jnp.swapaxes(rows, 0, 1)
-    grad_copies = tile_exchange(5, grad_out, grad_in)
-    grad_in[me] = grad_out[me]
+    grad_copies = tile_exchange(5, grad_out, grad_in, back=True)
+    grad_in[spot] = grad_out[me]
     finish(gather_copies)
     for f in range(2):
         for i in range(cols // LANES):
@@ -509,7 +576,7 @@
             vmem(parts - 1, span, 8, LANES),
             vmem(3, total, 8, LANES),
             vmem(parts - 1, 3, span, 8, LANES),
-            vmem(9 * 8 * (cols // WIN), WIN),
+            vmem(9 * 8 * (cols // BLOCK), BLOCK),
             vmem(strips, 6, 8, WIN),
             vmem(strips, 6, 8, WIN),
             vmem(strips, 8, WIN),
@@ -532,6 +599,10 @@
             pltpu.SemaphoreType.DMA((4, parts - 1)),
             pltpu.SemaphoreType.DMA((4, parts - 1)),
             pltpu.SemaphoreType.DMA((len(fields),)),
+            vmem(5, 2, 2, strips, LANES),
+            vmem(5, 2, 2, strips, LANES),
+            pltpu.SemaphoreType.DMA((5, 2)),
+            pltpu.SemaphoreType.DMA((5, 2)),
         ],
         compiler_params=pltpu.CompilerParams(
             collective_id=0, has_side_effects=True, vmem_limit_bytes=VMEM_LIMIT

time: 45.7 us -> 49.8 us (1.090)
  Pallas kernels: 42.6 us -> 46.7 us
    pallas_call x1, Pallas kernels: 42.6 us -> 46.7 us  [on_device(): pl.pallas_call(functools.partial(fused_kernel, strips, parts), out_shape=...]
where the time goes in v4:
time: 49.8 us; the launch traced here: 49.6 us
  Pallas kernels  46.7 us (94%)
  local copies, waits for them, and re-layouts  2.3 us (5%)
  between operations  0.65 us (1%)
    pallas_call x1, Pallas kernels, on_device(): pl.pallas_call(functools.partial(fused_kernel, strips, parts), out_shape=...  46.7 us
    unnamed x4, local copies, waits for them, and re-layouts  2.3 us

profile of v4, /device:TPU:0, one launch (start us, length us, event | category | flops | bytes accessed | tf_op | source)
XLA Modules:
  0.0 49.6 jit_solution(11686274221319693113)
XLA Ops:
  0.6 46.7 %shard_map.131 = (f32[2,8,3072]{2,1,0:T(8,128)}, f32[8,3072]{1,0:T(8,128)}) custom-call(f32[2,8,3072]{2,1,0:T(8,128)} %refs_0_.1, f32[4,8,3072]{2,1,0:T(8,128)} %refs_1_.1, f32[8,3072]{1,0:T(8,128)} %refs_2_.1, f32[8,3072]{1,0:T(8,128)} %refs_3_.1, s32[8,3072]{1,0:T(8,128)} %refs_4_.1, s32[8,3072]{1,0:T(8,128)} %refs_5_.1, f32[2,8,3072]{2,1,0:T(8,128)} %refs_6_.1, ...), custom_call_target="tpu_custom_call" | custom-call | tf_op jit(solution)/shard_map/pallas_call | solution.py:563
  47.3 0.0 copy-start
  47.3 1.7 %copy.16 = f32[2,8,3072]{2,1,0:T(8,128)} copy(f32[2,8,3072]{2,1,0:T(8,128)} %get-tuple-element.4) | data formatting | bytes 393216
  49.0 0.0 copy-done
  49.0 0.6 %copy.17 = f32[8,3072]{1,0:T(8,128)} copy(f32[8,3072]{1,0:T(8,128)S(1)} %copy-done) | data formatting | bytes 196608
Async XLA Ops:
  47.3 1.7 %copy-start = (f32[8,3072]{1,0:T(8,128)S(1)}, f32[8,3072]{1,0:T(8,128)}, u32[]{:S(2)}) copy-start(f32[8,3072]{1,0:T(8,128)} %get-tuple-element.5) | copy-start | bytes 294916

commit v5 on v3

--- a/solution.py
+++ b/solution.py
@@ -47,12 +47,34 @@
         acc_ref[...] += prod
 
 
+def split_columns(x):
+    source = lax.broadcasted_iota(jnp.int32, (WIN, WIN), 0)
+    target = lax.broadcasted_iota(jnp.int32, (WIN, WIN), 1)
+    wanted = jnp.where(target < LANES, 2 * target, 2 * target - WIN + 1)
+    pick = jnp.where(source == wanted, 1.0, 0.0)
+    return jnp.dot(
+        x, pick, precision=lax.Precision.HIGHEST, preferred_element_type=jnp.float32
+    )
+
+
+def own_columns(x):
+    source = lax.broadcasted_iota(jnp.int32, (WIN, LANES), 0)
+    target = lax.broadcasted_iota(jnp.int32, (WIN, LANES), 1)
+    column = jnp.where(source < LANES, 2 * source, 2 * source - WIN + 1)
+    pick = jnp.where(column == target + HALO, 1.0, 0.0)
+    return jnp.dot(
+        x, pick, precision=lax.Precision.HIGHEST, preferred_element_type=jnp.float32
+    )
+
+
 def east_of(x):
-    return pltpu.roll(x, WIN - 1, 1)
+    even, odd = x[:, :LANES], x[:, LANES:]
+    return jnp.concatenate([odd, pltpu.roll(even, LANES - 1, 1)], axis=1)
 
 
 def west_of(x):
-    return pltpu.roll(x, 1, 1)
+    even, odd = x[:, :LANES], x[:, LANES:]
+    return jnp.concatenate([pltpu.roll(odd, 1, 1), even], axis=1)
 
 
 def up(x):
@@ -83,15 +105,11 @@
             for f in range(2):
                 g = 1 - f
                 c = lambda k: coef[f, k, a]
-                new = c(0) * here[f][0] + force[f, a]
-                new = new + c(1) * after[f][0]
-                new = new + c(2) * before[f][0]
-                new = new + c(3) * here[f][1]
-                new = new + c(4) * here[f][2]
-                new = new + c(5) * after[g][1]
-                new = new + c(6) * after[g][2]
-                new = new + c(7) * before[g][1]
-                new = new + c(8) * before[g][2]
+                near = c(0) * here[f][0] + force[f, a]
+                near = near + (c(3) * here[f][1] + c(4) * here[f][2])
+                over = c(1) * after[f][0] + (c(5) * after[g][1] + c(6) * after[g][2])
+                under = c(2) * before[f][0] + (c(7) * before[g][1] + c(8) * before[g][2])
+                new = near + (over + under)
                 state[dst, f, a] = new
             before, here = here, after
 
@@ -329,6 +347,12 @@
         for t in range(strips):
             send_a[t, f] = cut_window(tiles, own, t)
 
+    def split_all(ref):
+        rows = ref[...].reshape(-1, WIN)
+        ref[...] = split_columns(rows).reshape(ref.shape)
+
+    split_all(send_a)
+
     def tile_exchange(n, out, into):
         return exchange(
             "tile",
@@ -362,6 +386,7 @@
         tiles.append(value)
     for t in range(strips):
         send_b[t] = cut_window(tiles, own, t)
+    split_all(send_b)
     b_copies = tile_exchange(2, send_b, recv_b)
     recv_b[me] = send_b[me]
 
@@ -417,16 +442,17 @@
             tiles.append(value)
         for t in range(strips):
             send_c[t, f] = cut_window(tiles, own, t)
+    split_all(send_c)
     c_copies = tile_exchange(3, send_c, recv_c)
     recv_c[me] = send_c[me]
     run_sweeps(state, coef, force, SWEEPS - EARLY)
 
-    def own_part(value):
-        return pltpu.roll(value, WIN - HALO, 1)[:, :LANES]
+    def own_rows(rows):
+        picked = own_columns(jnp.concatenate(rows, axis=0))
+        return jnp.swapaxes(picked.reshape(8, strips, LANES), 0, 1)
 
     for f in range(2):
-        parts_f = jnp.stack([own_part(state[0, f, a]) for a in range(8)], 0)
-        vel_out[:, f] = jnp.swapaxes(parts_f, 0, 1)
+        vel_out[:, f] = own_rows([state[0, f, a] for a in range(8)])
     vel_copies = tile_exchange(4, vel_out, vel_in)
     vel_in[me] = vel_out[me]
 
@@ -455,16 +481,12 @@
     gather_copies = layer_gather(2, vel_all)
     run_sweeps(state, coef, force, SWEEPS - RETURN)
 
-    rows = jnp.stack(
+    grad_out[...] = own_rows(
         [
-            own_part(
-                -(get(2, a) * (gain[0, a] * state[0, 0, a] + gain[1, a] * state[0, 1, a]))
-            )
+            -(get(2, a) * (gain[0, a] * state[0, 0, a] + gain[1, a] * state[0, 1, a]))
             for a in range(8)
-        ],
-        0,
-    )
-    grad_out[...] = jnp.swapaxes(rows, 0, 1)
+        ]
+    )
     grad_copies = tile_exchange(5, grad_out, grad_in)
     grad_in[me] = grad_out[me]
     finish(gather_copies)

time: 45.7 us -> 45.5 us (level)
  no operation moved by 1% of the time
where the time goes in v5:
time: 45.5 us; the launch traced here: 45.3 us
  Pallas kernels  42.4 us (93%)
  local copies, waits for them, and re-layouts  2.3 us (5%)
  between operations  0.65 us (1%)
    pallas_call x1, Pallas kernels, on_device(): pl.pallas_call(functools.partial(fused_kernel, strips, parts), out_shape=...  42.4 us
    unnamed x4, local copies, waits for them, and re-layouts  2.3 us

profile of v5, /device:TPU:0, one launch (start us, length us, event | category | flops | bytes accessed | tf_op | source)
XLA Modules:
  0.0 45.3 jit_solution(15349053936923304548)
XLA Ops:
  0.6 42.4 %shard_map.131 = (f32[2,8,3072]{2,1,0:T(8,128)}, f32[8,3072]{1,0:T(8,128)}) custom-call(f32[2,8,3072]{2,1,0:T(8,128)} %refs_0_.1, f32[4,8,3072]{2,1,0:T(8,128)} %refs_1_.1, f32[8,3072]{1,0:T(8,128)} %refs_2_.1, f32[8,3072]{1,0:T(8,128)} %refs_3_.1, s32[8,3072]{1,0:T(8,128)} %refs_4_.1, s32[8,3072]{1,0:T(8,128)} %refs_5_.1, f32[2,8,3072]{2,1,0:T(8,128)} %refs_6_.1, ...), custom_call_target="tpu_custom_call" | custom-call | tf_op jit(solution)/shard_map/pallas_call | solution.py:518
  43.0 0.0 copy-start
  43.1 1.7 %copy.16 = f32[2,8,3072]{2,1,0:T(8,128)} copy(f32[2,8,3072]{2,1,0:T(8,128)} %get-tuple-element.4) | data formatting | bytes 393216
  44.7 0.0 copy-done
  44.7 0.6 %copy.17 = f32[8,3072]{1,0:T(8,128)} copy(f32[8,3072]{1,0:T(8,128)S(1)} %copy-done) | data formatting | bytes 196608
Async XLA Ops:
  43.0 1.7 %copy-start = (f32[8,3072]{1,0:T(8,128)S(1)}, f32[8,3072]{1,0:T(8,128)}, u32[]{:S(2)}) copy-start(f32[8,3072]{1,0:T(8,128)} %get-tuple-element.5) | copy-start | bytes 294916

commit v6 on v5

--- a/solution.py
+++ b/solution.py
@@ -173,7 +173,6 @@
 
 
 MESH = pl.DeviceIdType.MESH
-EARLY = 4
 RETURN = 16
 
 
@@ -420,18 +419,6 @@
         layer_recv.at[1],
     )
 
-    finish(a_copies)
-    finish(b_copies)
-    for f in range(6):
-        x_ref[f] = jnp.swapaxes(recv_a[:, f], 0, 1)
-    x_ref[6] = jnp.swapaxes(recv_b[...], 0, 1)
-
-    def get(f, a):
-        return x_ref[f, a]
-
-    make_coefs(layers, get, state, coef, gain, force)
-    run_sweeps(state, coef, force, EARLY)
-
     finish(maps_copies)
     for f in range(3):
         tiles = []
@@ -445,7 +432,18 @@
     split_all(send_c)
     c_copies = tile_exchange(3, send_c, recv_c)
     recv_c[me] = send_c[me]
-    run_sweeps(state, coef, force, SWEEPS - EARLY)
+
+    finish(a_copies)
+    finish(b_copies)
+    for f in range(6):
+        x_ref[f] = jnp.swapaxes(recv_a[:, f], 0, 1)
+    x_ref[6] = jnp.swapaxes(recv_b[...], 0, 1)
+
+    def get(f, a):
+        return x_ref[f, a]
+
+    make_coefs(layers, get, state, coef, gain, force)
+    run_sweeps(state, coef, force, SWEEPS)
 
     def own_rows(rows):
         picked = own_columns(jnp.concatenate(rows, axis=0))
@@ -502,6 +500,29 @@
         grad_ref[:, i * LANES : (i + 1) * LANES] = grad_all[0, i]
 
 
+def hand_over(vel_ref, grad_ref, vel_out, grad_out, vel_held, grad_held, sems):
+    pieces = [
+        (vel_ref.at[0], vel_held.at[0], vel_out.at[0]),
+        (vel_ref.at[1], vel_held.at[1], vel_out.at[1]),
+        (grad_ref, grad_held, grad_out),
+    ]
+    loads = [
+        pltpu.make_async_copy(source, held, sems.at[0, n])
+        for n, (source, held, _) in enumerate(pieces)
+    ]
+    stores = [
+        pltpu.make_async_copy(held, target, sems.at[1, n])
+        for n, (_, held, target) in enumerate(pieces)
+    ]
+    for load in loads:
+        load.start()
+    for load, store in zip(loads, stores):
+        load.wait()
+        store.start()
+    for store in stores:
+        store.wait()
+
+
 def on_device(*fields):
     strips, parts = lax.axis_size("tile"), lax.axis_size("layer")
     cols = fields[2].shape[1]
@@ -515,7 +536,7 @@
     def vmem(*shape):
         return pltpu.VMEM(shape, jnp.float32)
 
-    return pl.pallas_call(
+    velocity, gradient = pl.pallas_call(
         functools.partial(fused_kernel, strips, parts),
         out_shape=(
             jax.ShapeDtypeStruct((2, 8, cols), jnp.float32),
@@ -559,6 +580,22 @@
             collective_id=0, has_side_effects=True, vmem_limit_bytes=VMEM_LIMIT
         ),
     )(*fields)
+    kept = (
+        jax.ShapeDtypeStruct(velocity.shape, jnp.float32),
+        jax.ShapeDtypeStruct(gradient.shape, jnp.float32),
+    )
+    return pl.pallas_call(
+        hand_over,
+        out_shape=kept,
+        in_specs=[pl.BlockSpec(memory_space=pl.ANY)] * 2,
+        out_specs=(pl.BlockSpec(memory_space=pl.ANY),) * 2,
+        scratch_shapes=[
+            vmem(*velocity.shape),
+            vmem(*gradient.shape),
+            pltpu.SemaphoreType.DMA((2, 3)),
+        ],
+        compiler_params=pltpu.CompilerParams(vmem_limit_bytes=VMEM_LIMIT),
+    )(velocity, gradient)
 
 
 def solution(mesh):

time: 45.5 us -> 45 us (0.989)
  local copies, waits for them, and re-layouts: 2.3 us -> 0 us
  Pallas kernels: 42.4 us -> 44.2 us
    unnamed x4 -> x0, local copies, waits for them, and re-layouts: 2.3 us -> none
    pallas_call x0 -> x1, Pallas kernels: none -> 1.68 us  [on_device(): pl.pallas_call(hand_over, out_shape=kept, in_specs=[pl.BlockSpec(memory_s...]
where the time goes in v6:
time: 45 us; the launch traced here: 44.8 us
  Pallas kernels  44.2 us (98%)
  between operations  0.64 us (1%)
    pallas_call x1, Pallas kernels, on_device(): pl.pallas_call(functools.partial(fused_kernel, strips, parts), out_shape=...  42.5 us
    pallas_call x1, Pallas kernels, on_device(): pl.pallas_call(hand_over, out_shape=kept, in_specs=[pl.BlockSpec(memory_s...  1.68 us

profile of v6, /device:TPU:0, one launch (start us, length us, event | category | flops | bytes accessed | tf_op | source)
XLA Modules:
  0.0 44.8 jit_solution(1763917552845968159)
XLA Ops:
  0.6 42.5 %shard_map.131 = (f32[2,8,3072]{2,1,0:T(8,128)}, f32[8,3072]{1,0:T(8,128)}) custom-call(f32[2,8,3072]{2,1,0:T(8,128)} %refs_0_.1, f32[4,8,3072]{2,1,0:T(8,128)} %refs_1_.1, f32[8,3072]{1,0:T(8,128)} %refs_2_.1, f32[8,3072]{1,0:T(8,128)} %refs_3_.1, s32[8,3072]{1,0:T(8,128)} %refs_4_.1, s32[8,3072]{1,0:T(8,128)} %refs_5_.1, f32[2,8,3072]{2,1,0:T(8,128)} %refs_6_.1, ...), custom_call_target="tpu_custom_call" | custom-call | tf_op jit(solution)/shard_map/pallas_call | solution.py:539
  43.1 1.7 %shard_map.132 = (f32[2,8,3072]{2,1,0:T(8,128)}, f32[8,3072]{1,0:T(8,128)}) custom-call(f32[2,8,3072]{2,1,0:T(8,128)} %get-tuple-element.4.vel_ref, f32[8,3072]{1,0:T(8,128)} %get-tuple-element.5.grad_ref), custom_call_target="tpu_custom_call" | custom-call | tf_op jit(solution)/shard_map/pallas_call | solution.py:587
